TPU v7x, 256 devices: a whole 4x4x8 slice. The times are simulated.
256 devices in a mesh: blk: 64 (over x_lo, z, y), grp: 4 (over x_hi, core).
Axes of the slice: x: 4 (x_hi: 2, x_lo: 2; x = x_hi * 2 + x_lo), y: 4, z: 8, core: 2. Of those that a mesh axis runs over, the one named last changes fastest.
Arguments:
- embedding: bfloat16 [131072, 256], P('blk'), may hold values from -1.5 to 1.5
- adjacency: int32 [4, 16384, 2048], P(None, 'blk', 'grp'), may hold values from 0 to 255
- owners: int32 [64], replicated, may hold values from 0 to 63, each once
Outputs:
- gradient: float32 [131072, 256], P(('blk', 'grp'))
Inputs may be any that keep to these rules, and one draw needn't show every extreme that they name: `owners`: entries 0 to 3 are distinct block indices; later entries are not read.
All inputs are finite; a program needn't handle non-finite values.
Results may differ from a plain program's by a relative error of at most 0.00044.
Values may be sent and summed in bfloat16 or wider, within the bound.
No kernel may reach another device: no remote copies, remote signals or barrier semaphores. Data moves between devices by JAX's collectives and lax.ppermute only.
A program may use at most 128 MiB of HBM per device.

v0:
```python
import jax
import jax.numpy as jnp
from jax import lax
from jax.sharding import PartitionSpec as P


def from_root(value, axis, source):
    kept = jnp.where(lax.axis_index(axis) == source, value, 0).astype(value.dtype)
    return lax.psum(kept, axis)


def body(embedding, adjacency, owners):
    rows = embedding.shape[0]
    width = embedding.shape[1]
    sections = adjacency.shape[0]
    groups = lax.axis_size("grp")
    quarter = rows // groups
    mine = lax.axis_index("blk")
    place = lax.axis_index("grp")
    own_part = lax.dynamic_slice_in_dim(embedding, place * quarter, quarter, 0)
    shifts = jnp.arange(8, dtype=jnp.int32)
    row_total = jnp.zeros((rows, width), jnp.float32)
    col_total = jnp.zeros((quarter, width), jnp.float32)
    for section in range(sections):
        block = from_root(own_part, "blk", owners[section])
        words = adjacency[section]
        bits = (
            (jnp.right_shift(words[:, None, :], shifts[None, :, None]) & 1)
            .reshape(rows, quarter)
            .astype(jnp.float32)
        )
        scores = jnp.einsum("rw,cw->rc", embedding, block, preferred_element_type=jnp.float32)
        error = (jax.nn.sigmoid(scores) - bits).astype(jnp.bfloat16)
        row_total = row_total + jnp.dot(error, block, preferred_element_type=jnp.float32)
        column = jnp.einsum("rc,rw->cw", error, embedding, preferred_element_type=jnp.float32)
        summed = lax.psum(column, "blk")
        col_total = col_total + jnp.where(mine == owners[section], summed, 0.0)
    rows_mine = lax.psum_scatter(row_total, "grp", scatter_dimension=0, tiled=True)
    return (rows_mine + col_total) * rows ** (-0.5)


def solution(mesh):
    return jax.shard_map(
        body,
        mesh=mesh,
        in_specs=(P("blk", None), P(None, "blk", "grp"), P()),
        out_specs=P(("blk", "grp"), None),
        check_vma=False,
    )
```

profile of v0, /device:TPU:32, one launch (start us, length us, event | category | flops | bytes accessed | tf_op | source)
XLA Modules:
  0.0 1297.4 jit_solution(17920324855088531389)
XLA Ops:
  6.5 0.0 all-reduce.7.cloned.1.call-start
  6.5 1.5 fusion.4
  10.5 2.0 broadcast_select_fusion
  12.6 0.0 all-reduce.7.cloned.1.call-update
  12.6 0.0 all-reduce.5.cloned.1.call-start
  12.6 0.1 shift_right_arithmetic.92
  12.8 1.7 slice_bitcast_fusion
  14.5 4.3 broadcast_bitcast_fusion
  18.8 5.4 copy.11
  24.2 5.4 copy.10
  29.6 4.4 broadcast_bitcast_fusion.2
  34.0 5.4 copy.9
  39.4 5.4 copy.8
  44.8 572.9 %all-reduce.7.cloned.1.call-done = (bf16[512,256]{1,0:T(8,128)(2,1)}, bf16[512,256]{1,0:T(8,128)(2,1)}, bf16[512,256]{1,0:T(8,128)(2,1)}, bf16[512,256]{1,0:T(8,128)(2,1)}) async-done(((bf16[512,256]{1,0:T(8,128)(2,1)}, bf16[512,256]{1,0:T(8,128)(2,1)}, bf16[512,256]{1,0:T(8,128)(2,1)}, bf16[512,256]{1,0:T(8,128)(2,1)}), (bf16[512,256]{1,0:T(8,128)(2,1)}, bf16[512,256]{1,0:T(8,128)(2,1)}, ...) | async-done | bytes 1048592 | tf_op jit(solution)/shard_map/psum | solution.py:9
  617.7 0.0 copy-start.12
  617.7 0.0 copy-start.5
  617.7 0.0 copy-start.10
  617.7 4.2 fusion
  621.9 0.0 copy-done.12
  621.9 1.5 fusion.9
  623.4 0.0 copy-done.5
  623.4 0.0 copy-done.10
  623.4 0.0 copy-start.7
  623.4 0.0 copy-start.11
  623.4 1.5 fusion.1
  624.9 0.0 copy-start
  624.9 1.6 fusion.8
  626.5 0.0 copy-done.7
  626.5 0.0 copy-done.11
  626.5 0.0 copy-start.6
  626.5 0.0 copy-start.8
  626.5 1.5 fusion.2
  628.0 0.0 copy-done
  628.1 0.0 copy-start.2
  628.1 1.6 fusion.7
  629.6 0.0 copy-done.6
  629.6 0.0 copy-done.8
  629.6 1.5 fusion.3
  631.2 0.0 copy-done.2
  631.2 0.0 copy-start.4
  631.2 1.3 copy-done.4
  632.5 1.5 fusion.6
  634.0 0.0 all-reduce.5.cloned.1.call-update
  634.0 0.2 reduce-scatter.2.cloned.1.call-start
  634.3 0.0 copy-start.3
  634.3 2.5 fusion.5
  636.8 0.0 copy-done.3
  636.8 0.0 copy-start.1
  636.8 0.8 convolution_add_fusion.2
  637.5 0.8 copy-done.1
  638.4 0.0 copy-start.9
  638.4 0.8 convolution_add_fusion.1
  639.1 0.2 copy-done.9
  639.3 2.1 convolution_add_fusion
  641.4 0.0 reduce-scatter.2.cloned.1.call-update
  641.4 600.3 %all-reduce.5.cloned.1.call-done = (f32[512,256]{1,0:T(8,128)}, f32[512,256]{1,0:T(8,128)}, f32[512,256]{1,0:T(8,128)}, f32[512,256]{1,0:T(8,128)}) async-done(((f32[512,256]{1,0:T(8,128)}, f32[512,256]{1,0:T(8,128)}, f32[512,256]{1,0:T(8,128)}, f32[512,256]{1,0:T(8,128)}), (f32[512,256]{1,0:T(8,128)}, f32[512,256]{1,0:T(8,128)}, f32[512,256]{1,0:T(8,128)}, ...) | async-done | bytes 2097168 | tf_op jit(solution)/shard_map/psum | solution.py:36
  1241.8 47.1 %reduce-scatter.2.cloned.1.call-done = f32[512,256]{1,0:T(8,128)} async-done(((f32[2048,256]{1,0:T(8,128)}), f32[512,256]{1,0:T(8,128)}) %reduce-scatter.2.cloned.1.call-update) | async-done | bytes 524304 | tf_op jit(solution)/shard_map/reduce_scatter | solution.py:38
  1288.9 2.0 add_multiply_fusion
  (1 shorter events, 0.0 us)
Async XLA Ops:
  6.5 611.1 %all-reduce.7.cloned.1.call-start = ((), (), s32[]{:S(2)}) async-start(), calls=%async_computation.3 | async-start | bytes 2097152 | tf_op jit(solution)/shard_map/psum | solution.py:9
  12.6 1229.2 %all-reduce.5.cloned.1.call-start = ((), (), s32[]{:S(2)}) async-start(), calls=%async_computation.2 | async-start | bytes 4194304 | tf_op jit(solution)/shard_map/psum | solution.py:36
  617.7 4.2 copy-start.12
  617.7 5.7 copy-start.5
  617.7 5.7 copy-start.10
  623.4 3.1 copy-start.7
  623.4 3.1 copy-start.11
  624.9 3.1 copy-start
  626.5 3.1 copy-start.6
  626.5 3.1 copy-start.8
  628.1 3.1 copy-start.2
  631.2 1.3 copy-start.4
  634.0 654.8 %reduce-scatter.2.cloned.1.call-start = ((), (), s32[]{:S(2)}) async-start(), calls=%async_computation.1 | async-start | bytes 2621440 | tf_op jit(solution)/shard_map/reduce_scatter | solution.py:38
  634.3 2.5 copy-start.3
  636.8 1.6 copy-start.1
  638.4 0.9 copy-start.9
Sparse Core Ops, SparseCore 0:
  12.7 604.9 all-reduce.6
  634.2 607.5 all-reduce.4
  1244.5 44.2 reduce-scatter.1
where the time goes:
time: 1300 us
  waiting for transfers between devices  1220 us (94%)
  local copies, waits for them, and re-layouts  36 us (3%)
  matrix products  21 us (2%)
  between operations  15.8 us (1%)
    psum x1, waiting for transfers between devices, body(): summed = lax.psum(column, 'blk')  600 us
    psum x1, waiting for transfers between devices, from_root(): return lax.psum(kept, axis)  573 us
    reduce_scatter x1, waiting for transfers between devices, body(): lax.psum_scatter(row_total, 'grp', scatter_dimension=0, tiled=True)  47.1 us
    shift_right_arithmetic x9, local copies, waits for them, and re-layouts, body(): jnp.right_shift(words[:, None, :], shifts[None, :, None]) & 1  32.1 us
  transfers between devices with their start and end apart: 3, of which 3 were waited for; matrix products, arithmetic and copies ran while one was open for 3% of the time, Pallas kernels for 0%

commit v1 on v0

v1 whole, which is shorter than its diff:
```python
import functools

import jax
import jax.numpy as jnp
from jax import lax
from jax.experimental import pallas as pl
from jax.experimental.pallas import tpu as pltpu
from jax.sharding import PartitionSpec as P

TILE = 256
PLANES = 8
WORDS = TILE // PLANES
VMEM_LIMIT = 48 * 1024 * 1024


def arrange_kernel(emb_ref, rows_ref, cols_ref):
    new = lax.broadcasted_iota(jnp.int32, (TILE, TILE), 0)
    old = lax.broadcasted_iota(jnp.int32, (TILE, TILE), 1)
    pick = old == (new & (WORDS - 1)) * PLANES + new // WORDS
    order = jnp.where(pick, 1.0, 0.0).astype(jnp.bfloat16)
    for tile in range(emb_ref.shape[0] // TILE):
        span = slice(tile * TILE, (tile + 1) * TILE)
        moved = jnp.dot(order, emb_ref[span, :], preferred_element_type=jnp.float32)
        rows_ref[span, :] = moved.astype(jnp.bfloat16)
        cols_ref[:, span] = moved.T.astype(jnp.bfloat16)


def half_kernel(first, *refs):
    if first:
        half_ref, rows_ref, cols_ref, block_ref, words_ref, row_ref, col_ref = refs
        prior_ref = None
    else:
        half_ref, rows_ref, cols_ref, block_ref, words_ref, prior_ref, row_ref, col_ref = refs
    sections = words_ref.shape[0]
    wide = block_ref.shape[0]
    each = wide // sections
    start = pl.multiple_of(half_ref[0] * each, each)
    block = block_ref[...]
    halved = block * jnp.bfloat16(0.5)
    for tile in range(rows_ref.shape[0] // TILE):
        span = slice(tile * TILE, (tile + 1) * TILE)
        here = rows_ref[span, :]
        scores = lax.dot_general(
            here, halved, (((1,), (1,)), ((), ())), preferred_element_type=jnp.float32
        )
        parts = []
        for section in range(sections):
            words = words_ref[section, pl.ds(tile * WORDS, WORDS), pl.ds(start, each)]
            planes = []
            for plane in range(PLANES):
                part = scores[plane * WORDS : (plane + 1) * WORDS, section * each : (section + 1) * each]
                sign = jnp.where((words & (1 << plane)) == 0, 1.0, -1.0)
                planes.append((jnp.tanh(part) + sign).astype(jnp.bfloat16))
            parts.append(jnp.concatenate(planes, axis=0))
        error = jnp.concatenate(parts, axis=1)
        row = jnp.dot(error, block, preferred_element_type=jnp.float32)
        if prior_ref is not None:
            row = row + prior_ref[span, :]
        row_ref[span, :] = row
        col = jnp.dot(cols_ref[:, span], error, preferred_element_type=jnp.float32)
        if tile == 0:
            col_ref[...] = col
        else:
            col_ref[...] += col


def vmem(count):
    return [pl.BlockSpec(memory_space=pltpu.VMEM)] * count


def arrange(embedding):
    rows, width = embedding.shape
    return pl.pallas_call(
        arrange_kernel,
        out_shape=(
            jax.ShapeDtypeStruct((rows, width), jnp.bfloat16),
            jax.ShapeDtypeStruct((width, rows), jnp.bfloat16),
        ),
        in_specs=vmem(1),
        out_specs=tuple(vmem(2)),
        compiler_params=pltpu.CompilerParams(vmem_limit_bytes=VMEM_LIMIT),
    )(embedding)


def half_products(half, by_row, by_col, block, words, prior):
    rows, width = by_row.shape
    wide = block.shape[0]
    first = prior is None
    args = (half, by_row, by_col, block, words) + (() if first else (prior,))
    flops = 3 * 2 * rows * wide * width
    return pl.pallas_call(
        functools.partial(half_kernel, first),
        out_shape=(
            jax.ShapeDtypeStruct((rows, width), jnp.float32),
            jax.ShapeDtypeStruct((width, wide), jnp.float32),
        ),
        in_specs=[pl.BlockSpec(memory_space=pltpu.SMEM)] + vmem(len(args) - 1),
        out_specs=tuple(vmem(2)),
        cost_estimate=pl.CostEstimate(flops=flops, bytes_accessed=8 << 20, transcendentals=rows * wide),
        compiler_params=pltpu.CompilerParams(vmem_limit_bytes=VMEM_LIMIT),
    )(*args)


def body(embedding, adjacency, owners):
    rows, width = embedding.shape
    sections = adjacency.shape[0]
    groups = lax.axis_size("grp")
    blocks = lax.axis_size("blk")
    quarter = rows // groups
    near = blocks // 2
    mine = lax.axis_index("blk")
    place = lax.axis_index("grp")
    side = mine // near
    core = place % 2
    high = place // 2
    flip_side = [(b, (b + near) % blocks) for b in range(blocks)]
    planes_zy = [list(range(x * near, (x + 1) * near)) for x in range(2)]

    own = lax.dynamic_slice_in_dim(embedding, place * quarter, quarter, 0)
    piece = quarter // blocks
    got = lax.all_to_all(own.reshape(blocks, piece, width), "blk", 0, 0)
    picked = jnp.stack([lax.dynamic_index_in_dim(got, owners[s], 0, keepdims=False) for s in range(sections)])
    spread = jnp.broadcast_to(picked[None], (near,) + picked.shape)
    half = lax.all_to_all(spread, "blk", 0, 0, axis_index_groups=planes_zy)
    near_block = half.transpose(1, 0, 2, 3).reshape(sections * quarter // 2, width)
    far_block = lax.ppermute(near_block, "blk", flip_side)

    by_row, by_col = arrange(embedding)
    row, near_col = half_products(side.reshape(1), by_row, by_col, near_block, adjacency, None)
    sent_col = lax.ppermute(near_col, "blk", flip_side)
    row, far_col = half_products(1 - side.reshape(1), by_row, by_col, far_block, adjacency, row)

    row = row.reshape(2, 2, quarter, width)
    away = lax.dynamic_index_in_dim(row, 1 - core, 1, keepdims=False)
    kept = lax.dynamic_index_in_dim(row, core, 1, keepdims=False)
    kept = kept + lax.ppermute(away, "grp", [(g, g ^ 1) for g in range(groups)])
    away = lax.dynamic_index_in_dim(kept, 1 - high, 0, keepdims=False)
    mine_row = lax.dynamic_index_in_dim(kept, high, 0, keepdims=False)
    mine_row = mine_row + lax.ppermute(away, "grp", [(g, g ^ 2) for g in range(groups)])

    col = (far_col + sent_col).reshape(near, width // near, sections * quarter // 2)
    col = lax.all_to_all(col, "blk", 0, 0, axis_index_groups=planes_zy)
    col = col.sum(axis=0).reshape(width // near, sections, quarter // 2)
    target = jnp.arange(blocks, dtype=jnp.int32)
    out = jnp.zeros((blocks, width // near, quarter // 2), jnp.float32)
    for s in range(sections):
        out = jnp.where((target == owners[s])[:, None, None], col[:, s][None], out)
    back = lax.all_to_all(out, "blk", 0, 0)
    back = back.reshape(2, width, quarter // 2)[::-1]
    owned = jnp.any(owners[:sections] == mine)
    side_col = back.transpose(0, 2, 1).reshape(quarter, width)
    mine_row = mine_row.reshape(quarter // TILE, PLANES, WORDS, width).transpose(0, 2, 1, 3).reshape(quarter, width)
    return (mine_row + jnp.where(owned, side_col, 0.0)) * (0.5 * rows ** (-0.5))


def solution(mesh):
    return jax.shard_map(
        body,
        mesh=mesh,
        in_specs=(P("blk", None), P(None, "blk", "grp"), P()),
        out_specs=P(("blk", "grp"), None),
        check_vma=False,
    )
```

time: 1300 us -> 167 us (0.13)
  waiting for transfers between devices: 1220 us -> 88.3 us
  starting transfers between devices: 0.27 us -> 38.6 us
  local copies, waits for them, and re-layouts: 36 us -> 9.34 us
  matrix products: 21 us -> 0 us
    psum x2 -> x0, waiting for transfers between devices: 1170 us -> none  [the longest x1 600 us: body(): summed = lax.psum(column, 'blk')]
    reduce_scatter x1 -> x0, waiting for transfers between devices: 47.1 us -> none  [body(): lax.psum_scatter(row_total, 'grp', scatter_dimension=0, tiled=True)]
    ppermute x0 -> x4, waiting for transfers between devices: none -> 45.3 us  [the longest x1 30.8 us: body(): far_block = lax.ppermute(near_block, 'blk', flip_side)]
    all_to_all x0 -> x4, waiting for transfers between devices: none -> 43 us  [the longest x1 22.7 us: body(): col = lax.all_to_all(col, 'blk', 0, 0, axis_index_groups=planes_zy)]
    all_to_all x0 -> x4, starting transfers between devices: none -> 33.8 us  [the longest x1 12.7 us: body(): got = lax.all_to_all(own.reshape(blocks, piece, width), 'blk', 0, 0)]
    shift_right_arithmetic x9 -> x0, local copies, waits for them, and re-layouts: 32.1 us -> none  [body(): jnp.right_shift(words[:, None, :], shifts[None, :, None]) & 1]
    dot_general x12 -> x0, matrix products: 21 us -> none  [the longest x4 8.73 us: body(): jnp.einsum('rw,cw->rc', embedding, block, preferred_element_type=jnp.floa...]
  transfers between devices with their start and end apart: 3 -> 8, of which waited for: 3 -> 5; matrix products, arithmetic and copies ran while one was open for 3% -> 5% of each run, Pallas kernels for 0% -> 4%
where the time goes in v1:
time: 167 us; the launch traced here: 165 us
  waiting for transfers between devices  88.3 us (53%)
  starting transfers between devices  38.6 us (23%)
  Pallas kernels  11.6 us (7%)
  other arithmetic  9.62 us (6%)
  local copies, waits for them, and re-layouts  9.34 us (6%)
  between operations  7.73 us (5%)
    ppermute x1, waiting for transfers between devices, body(): far_block = lax.ppermute(near_block, 'blk', flip_side)  30.8 us
    all_to_all x1, waiting for transfers between devices, body(): col = lax.all_to_all(col, 'blk', 0, 0, axis_index_groups=planes_zy)  22.7 us
    all_to_all x1, waiting for transfers between devices, body(): half = lax.all_to_all(spread, 'blk', 0, 0, axis_index_groups=planes_zy)  16.2 us
    ppermute x1, waiting for transfers between devices, body(): lax.ppermute(away, 'grp', [(g, g ^ 2) for g in range(groups)])  14.5 us
    all_to_all x1, starting transfers between devices, body(): got = lax.all_to_all(own.reshape(blocks, piece, width), 'blk', 0, 0)  12.7 us
    pallas_call x2, Pallas kernels, half_products(): pl.pallas_call(functools.partial(half_kernel, first), out_shape=(jax.Shap...  11.1 us
    all_to_all x1, starting transfers between devices, body(): back = lax.all_to_all(out, 'blk', 0, 0)  7.84 us
    all_to_all x1, starting transfers between devices, body(): col = lax.all_to_all(col, 'blk', 0, 0, axis_index_groups=planes_zy)  7.51 us
  transfers between devices with their start and end apart: 8, of which 5 were waited for; matrix products, arithmetic and copies ran while one was open for 5% of the time, Pallas kernels for 4%

profile of v1, /device:TPU:32, one launch (start us, length us, event | category | flops | bytes accessed | tf_op | source)
XLA Modules:
  0.0 165.3 jit_solution(11580644515603026730)
XLA Ops:
  0.0 0.0 copy-start
  0.0 1.8 %dynamic-slice_bitcast_fusion.2 = bf16[64,8,256]{2,1,0:T(8,128)(2,1)} fusion(bf16[2048,256]{1,0:T(8,128)(2,1)} %emb_ref.1, s32[]{:T(128)S(6)} %select_n.72), kind=kLoop, calls=%fused_computation.9 | loop fusion | bytes 524292 | tf_op jit(solution)/shard_map/reshape | solution.py:121
  1.8 12.7 %all-to-all-start = ((bf16[64,8,256]{2,1,0:T(8,128)(2,1)}), bf16[64,8,256]{2,1,0:T(8,128)(2,1)S(1)}, u32[]{:S(2)}, u32[]{:S(2)}) async-start(bf16[64,8,256]{2,1,0:T(8,128)(2,1)} %dynamic-slice_bitcast_fusion.2), calls=%async_computation | async-start | bytes 524288 | tf_op jit(solution)/shard_map/all_to_all | solution.py:121
  14.5 1.5 fusion.1
  23.4 4.1 %all-to-all-done = bf16[64,8,256]{2,1,0:T(8,128)(2,1)S(1)} async-done(((bf16[64,8,256]{2,1,0:T(8,128)(2,1)}), bf16[64,8,256]{2,1,0:T(8,128)(2,1)S(1)}, u32[]{:S(2)}, u32[]{:S(2)}) %all-to-all-start) | async-done | bytes 262176 | tf_op jit(solution)/shard_map/all_to_all | solution.py:121
  27.6 0.9 broadcast_in_dim.71
  28.4 5.7 %all-to-all-start.1 = ((bf16[32,4,8,256]{3,2,1,0:T(8,128)(2,1)}), bf16[32,4,8,256]{3,2,1,0:T(8,128)(2,1)}, u32[]{:S(2)}, u32[]{:S(2)}) async-start(bf16[32,4,8,256]{3,2,1,0:T(8,128)(2,1)} %broadcast_in_dim.71), calls=%async_computation.1 | async-start | bytes 1048576 | tf_op jit(solution)/shard_map/all_to_all | solution.py:124
  34.2 0.0 copy-done
  34.2 0.5 shard_map.37
  34.7 0.0 copy-start.1
  34.8 16.2 %all-to-all-done.1 = bf16[32,4,8,256]{3,2,1,0:T(8,128)(2,1)} async-done(((bf16[32,4,8,256]{3,2,1,0:T(8,128)(2,1)}), bf16[32,4,8,256]{3,2,1,0:T(8,128)(2,1)}, u32[]{:S(2)}, u32[]{:S(2)}) %all-to-all-start.1) | async-done | bytes 524320 | tf_op jit(solution)/shard_map/all_to_all | solution.py:124
  50.9 1.1 copy.6
  52.0 5.2 %shard_map.38 = (f32[2048,256]{1,0:T(8,128)S(1)}, f32[256,1024]{1,0:T(8,128)S(1)}) custom-call(s32[1]{0:T(128)} %bitcast.refs_0_, bf16[2048,256]{1,0:T(8,128)(2,1)S(1)} %get-tuple-element.11.refs_1_, bf16[256,2048]{1,0:T(8,128)(2,1)S(1)} %get-tuple-element.12.refs_2_, bf16[1024,256]{1,0:T(8,128)(2,1)S(1)} %bitcast.43, s32[4,256,512]{2,1,0:T(8,128)} %refs_4_.3), custom_call_target="tpu_custom_call" | custom-call | flops 3221225472 | bytes 8388608 | tf_op jit(solution)/shard_map/pallas_call | solution.py:91
  57.2 0.0 copy-done.1
  57.2 0.0 copy-start.3
  57.2 1.3 copy-done.3
  58.5 1.7 %collective-permute-start.3 = (f32[256,1024]{1,0:T(8,128)S(1)}, f32[256,1024]{1,0:T(8,128)S(1)}, u32[]{:S(2)}, u32[]{:S(2)}) collective-permute-start(f32[256,1024]{1,0:T(8,128)S(1)} %get-tuple-element.16), channel_id=1, source_target_pairs={{0,128},{4,132},{8,136},{12,140},{16,144},{20,148},{24,152},{28,15... | collective-permute-start | bytes 3145736 | tf_op jit(solution)/shard_map/ppermute | solution.py:130
  60.3 0.3 collective-permute-start
  60.6 30.8 %collective-permute-done.refs_3_ = bf16[1024,256]{1,0:T(8,128)(2,1)S(1)} collective-permute-done((bf16[1024,256]{1,0:T(8,128)(2,1)S(1)}, bf16[1024,256]{1,0:T(8,128)(2,1)S(1)}, u32[]{:S(2)}, u32[]{:S(2)}) %collective-permute-start) | collective-permute-done | bytes 524320 | tf_op jit(solution)/shard_map/ppermute | solution.py:126
  91.4 0.0 copy-start.2
  91.4 1.2 copy-done.2
  92.6 5.9 %shard_map.39 = (f32[2048,256]{1,0:T(8,128)S(1)}, f32[256,1024]{1,0:T(8,128)S(1)}) custom-call(s32[1]{0:T(128)S(6)} %sub.17.refs_0_, bf16[2048,256]{1,0:T(8,128)(2,1)S(1)} %get-tuple-element.11.refs_1_, bf16[256,2048]{1,0:T(8,128)(2,1)S(1)} %copy-done.2, bf16[1024,256]{1,0:T(8,128)(2,1)S(1)} %collective-permute-done.refs_3_, s32[4,256,512]{2,1,0:T(8,128)} %refs_4_.3, ...), custom_call_target="tpu_custom_call" | custom-call | flops 3221225472 | bytes 8388608 | tf_op jit(solution)/shard_map/pallas_call | solution.py:91
  98.6 0.0 collective-permute-done.3
  98.6 1.1 add_bitcast_fusion
  99.7 7.5 %all-to-all-start.2 = ((f32[32,8,1024]{2,1,0:T(8,128)}), f32[32,8,1024]{2,1,0:T(8,128)S(1)}, u32[]{:S(2)}, u32[]{:S(2)}) async-start(f32[32,8,1024]{2,1,0:T(8,128)} %add_bitcast_fusion), calls=%async_computation.2 | async-start | bytes 2097152 | tf_op jit(solution)/shard_map/all_to_all | solution.py:142
  107.2 1.1 dynamic-slice_bitcast_fusion
  108.3 0.0 collective-permute-start.1
  108.3 1.2 iota_compare_fusion
  109.5 1.3 iota_compare_fusion.2
  110.8 22.7 %all-to-all-done.2 = f32[32,8,1024]{2,1,0:T(8,128)S(1)} async-done(((f32[32,8,1024]{2,1,0:T(8,128)}), f32[32,8,1024]{2,1,0:T(8,128)S(1)}, u32[]{:S(2)}, u32[]{:S(2)}) %all-to-all-start.2) | async-done | bytes 1048608 | tf_op jit(solution)/shard_map/all_to_all | solution.py:142
  133.5 0.1 reduce_sum.9
  133.6 1.1 select_select_fusion
  134.7 7.8 %all-to-all-start.3 = ((f32[64,8,256]{2,1,0:T(8,128)}), f32[64,8,256]{2,1,0:T(8,128)}, u32[]{:S(2)}, u32[]{:S(2)}) async-start(f32[64,8,256]{2,1,0:T(8,128)} %select_select_fusion), calls=%async_computation.3 | async-start | bytes 1048576 | tf_op jit(solution)/shard_map/all_to_all | solution.py:148
  142.6 0.0 copy-start.4
  142.6 0.0 collective-permute-done.1
  142.6 1.4 bitcast_add_fusion
  144.0 2.8 %collective-permute-start.2 = (f32[512,256]{1,0:T(8,128)S(1)}, f32[512,256]{1,0:T(8,128)S(1)}, u32[]{:S(2)}, u32[]{:S(2)}) collective-permute-start(f32[512,256]{1,0:T(8,128)S(1)} %dynamic-slice_bitcast_fusion.1), channel_id=1, source_target_pairs={{0,2},{1,3},{2,0},{3,1},{4,6},{5,7},{6,4},{7,5},{8,10},{9,11},{10,... | collective-permute-start | bytes 1572872 | tf_op jit(solution)/shard_map/ppermute | solution.py:139
  146.8 0.0 copy-done.4
  146.8 0.7 compare_reduce_fusion
  147.5 14.5 %collective-permute-done.2 = f32[512,256]{1,0:T(8,128)S(1)} collective-permute-done((f32[512,256]{1,0:T(8,128)S(1)}, f32[512,256]{1,0:T(8,128)S(1)}, u32[]{:S(2)}, u32[]{:S(2)}) %collective-permute-start.2) | collective-permute-done | bytes 524320 | tf_op jit(solution)/shard_map/ppermute | solution.py:139
  162.0 0.1 bitcast_add_fusion.2
  162.1 0.3 copy.7
  162.4 0.0 all-to-all-done.3
  162.4 1.8 %select_bitcast_fusion = f32[2,256,256]{1,2,0:T(8,128)S(1)} fusion(f32[2,256,256]{2,1,0:T(8,128)} %bitcast.22, pred[]{:T(512)} %compare_reduce_fusion), kind=kLoop, calls=%fused_computation.6 | loop fusion | flops 131072 | bytes 1048577 | tf_op jit(solution)/shard_map/jit(_where)/select_n | solution.py:153
  164.2 0.2 copy.8
  164.4 0.9 fusion
  (4 shorter events, 0.1 us)
Async XLA Ops:
  0.0 34.2 %copy-start = (bf16[2048,256]{1,0:T(8,128)(2,1)S(1)}, bf16[2048,256]{1,0:T(8,128)(2,1)}, u32[]{:S(2)}) copy-start(bf16[2048,256]{1,0:T(8,128)(2,1)} %emb_ref.1) | copy-start | bytes 3145732
  1.8 25.8 %all-to-all-start = ((bf16[64,8,256]{2,1,0:T(8,128)(2,1)}), bf16[64,8,256]{2,1,0:T(8,128)(2,1)S(1)}, u32[]{:S(2)}, u32[]{:S(2)}) async-start(bf16[64,8,256]{2,1,0:T(8,128)(2,1)} %dynamic-slice_bitcast_fusion.2), calls=%async_computation | async-start | bytes 524288 | tf_op jit(solution)/shard_map/all_to_all | solution.py:121
  28.4 22.5 %all-to-all-start.1 = ((bf16[32,4,8,256]{3,2,1,0:T(8,128)(2,1)}), bf16[32,4,8,256]{3,2,1,0:T(8,128)(2,1)}, u32[]{:S(2)}, u32[]{:S(2)}) async-start(bf16[32,4,8,256]{3,2,1,0:T(8,128)(2,1)} %broadcast_in_dim.71), calls=%async_computation.1 | async-start | bytes 1048576 | tf_op jit(solution)/shard_map/all_to_all | solution.py:124
  34.7 22.5 %copy-start.1 = (bf16[256,2048]{1,0:T(8,128)(2,1)}, bf16[256,2048]{1,0:T(8,128)(2,1)S(1)}, u32[]{:S(2)}) copy-start(bf16[256,2048]{1,0:T(8,128)(2,1)S(1)} %get-tuple-element.12.refs_2_) | copy-start | bytes 3145732
  57.2 1.3 copy-start.3
  58.5 40.0 %collective-permute-start.3 = (f32[256,1024]{1,0:T(8,128)S(1)}, f32[256,1024]{1,0:T(8,128)S(1)}, u32[]{:S(2)}, u32[]{:S(2)}) collective-permute-start(f32[256,1024]{1,0:T(8,128)S(1)} %get-tuple-element.16), channel_id=1, source_target_pairs={{0,128},{4,132},{8,136},{12,140},{16,144},{20,148},{24,152},{28,15... | collective-permute-start | bytes 3145736 | tf_op jit(solution)/shard_map/ppermute | solution.py:130
  60.3 31.1 %collective-permute-start = (bf16[1024,256]{1,0:T(8,128)(2,1)S(1)}, bf16[1024,256]{1,0:T(8,128)(2,1)S(1)}, u32[]{:S(2)}, u32[]{:S(2)}) collective-permute-start(bf16[1024,256]{1,0:T(8,128)(2,1)S(1)} %bitcast.44), channel_id=1, source_target_pairs={{0,128},{4,132},{8,136},{12,140},{16,144},{20,148},{24,152},{28,15... | collective-permute-start | bytes 1572872 | tf_op jit(solution)/shard_map/ppermute | solution.py:126
  91.4 1.2 copy-start.2
  99.7 33.8 %all-to-all-start.2 = ((f32[32,8,1024]{2,1,0:T(8,128)}), f32[32,8,1024]{2,1,0:T(8,128)S(1)}, u32[]{:S(2)}, u32[]{:S(2)}) async-start(f32[32,8,1024]{2,1,0:T(8,128)} %add_bitcast_fusion), calls=%async_computation.2 | async-start | bytes 2097152 | tf_op jit(solution)/shard_map/all_to_all | solution.py:142
  108.3 34.3 %collective-permute-start.1 = (f32[2,512,256]{2,1,0:T(8,128)}, f32[2,512,256]{2,1,0:T(8,128)}, u32[]{:S(2)}, u32[]{:S(2)}) collective-permute-start(f32[2,512,256]{2,1,0:T(8,128)} %dynamic-slice_bitcast_fusion), channel_id=1, source_target_pairs={{0,1},{1,0},{2,3},{3,2},{4,5},{5,4},{6,7},{7,6},{8,9},{9,8},{10,11... | collective-permute-start | bytes 3145736 | tf_op jit(solution)/shard_map/ppermute | solution.py:136
  134.7 27.7 %all-to-all-start.3 = ((f32[64,8,256]{2,1,0:T(8,128)}), f32[64,8,256]{2,1,0:T(8,128)}, u32[]{:S(2)}, u32[]{:S(2)}) async-start(f32[64,8,256]{2,1,0:T(8,128)} %select_select_fusion), calls=%async_computation.3 | async-start | bytes 1048576 | tf_op jit(solution)/shard_map/all_to_all | solution.py:148
  142.6 4.2 %copy-start.4 = (s32[64]{0:T(128)S(1)}, s32[64]{0:T(128)}, u32[]{:S(2)}) copy-start(s32[64]{0:T(128)} %param.5) | copy-start | bytes 772
  144.0 18.0 %collective-permute-start.2 = (f32[512,256]{1,0:T(8,128)S(1)}, f32[512,256]{1,0:T(8,128)S(1)}, u32[]{:S(2)}, u32[]{:S(2)}) collective-permute-start(f32[512,256]{1,0:T(8,128)S(1)} %dynamic-slice_bitcast_fusion.1), channel_id=1, source_target_pairs={{0,2},{1,3},{2,0},{3,1},{4,6},{5,7},{6,4},{7,5},{8,10},{9,11},{10,... | collective-permute-start | bytes 1572872 | tf_op jit(solution)/shard_map/ppermute | solution.py:139

commit v2 on v0

v2 whole, which is shorter than its diff:
```python
import functools

import jax
import jax.numpy as jnp
from jax import lax
from jax.experimental import pallas as pl
from jax.experimental.pallas import tpu as pltpu
from jax.sharding import PartitionSpec as P

TILE = 256
PLANES = 8
WORDS = TILE // PLANES
SECTIONS = 4
LINE = 8

ANYWHERE = pl.BlockSpec(memory_space=pltpu.HBM)
SCALARS = pl.BlockSpec(memory_space=pltpu.SMEM)
VECTORS = pl.BlockSpec(memory_space=pltpu.VMEM)


def local_call(kernel, outs, ins, scratch=(), cost=None, limit=32):
    return pl.pallas_call(
        kernel,
        out_shape=outs,
        in_specs=ins,
        out_specs=jax.tree.map(lambda _: VECTORS, outs),
        scratch_shapes=scratch,
        cost_estimate=cost,
        compiler_params=pltpu.CompilerParams(vmem_limit_bytes=limit << 20),
    )


def own_kernel(owners_ref, emb_ref, own_ref, list_ref, held_ref, sem):
    blocks, deep, lanes = own_ref.shape
    quarter, width = held_ref.shape
    start = lax.axis_index("grp") * quarter
    rows = pl.ds(pl.multiple_of(start, quarter), quarter)
    copy = pltpu.make_async_copy(emb_ref.at[rows, :], held_ref, sem.at[0])
    names = pltpu.make_async_copy(owners_ref, list_ref, sem.at[1])
    copy.start()
    names.start()
    copy.wait()
    chunks = quarter // deep
    for part in range(width // lanes):
        for chunk in range(chunks):
            own_ref[part * chunks + chunk] = held_ref[
                chunk * deep : (chunk + 1) * deep, part * lanes : (part + 1) * lanes
            ]
    names.wait()


def to_line_kernel(owners_ref, got_ref, sent_ref):
    for s in range(SECTIONS):
        held = got_ref[owners_ref[s]]
        for part in range(sent_ref.shape[0]):
            sent_ref[part, s] = held


def to_plane_kernel(came_ref, sent_ref):
    held = came_ref[...]
    for part in range(sent_ref.shape[0]):
        sent_ref[part] = held


def products_kernel(
    emb_ref, pieces_ref, far_words_ref, keep_ref, send_ref, col_ref,
    block_ref, halved_ref, rows_ref, cols_ref, error_ref, words_ref, sem,
):
    plane, line, sections, deep, lanes = pieces_ref.shape
    rows, width = emb_ref.shape
    fetch = pltpu.make_async_copy(far_words_ref, words_ref, sem)
    fetch.start()
    quarter = rows // 4
    place = lax.axis_index("grp")
    core, high = place % 2, place // 2
    for section in range(sections):
        for z in range(line):
            for xy in range(plane):
                at = section * quarter + (z * 4 + xy % 4) * deep
                span = slice(at, at + deep)
                cut = slice(xy // 4 * lanes, (xy // 4 + 1) * lanes)
                value = pieces_ref[xy, z, section]
                block_ref[span, cut] = value
                halved_ref[span, cut] = value * jnp.bfloat16(0.5)

    new = lax.broadcasted_iota(jnp.int32, (TILE, TILE), 0)
    old = lax.broadcasted_iota(jnp.int32, (TILE, TILE), 1)
    pick = old == (new % WORDS) * PLANES + new // WORDS
    order = jnp.where(pick, 1.0, 0.0).astype(jnp.bfloat16)
    source = (new // 128) * 128 + (new // 4 % 8) * 16 + (new // 32 % 4) * 4 + new % 4
    spread = jnp.where(old == source, 1.0, 0.0).astype(jnp.bfloat16)

    tiles = []
    for away in (1, 0):
        for other in (0, 1):
            for sub in range(2):
                tiles.append(((high ^ other) * 2 + (core ^ away)) * 2 + sub)
    for step, tile in enumerate(tiles):
        span = slice(step * TILE, (step + 1) * TILE)
        raw = emb_ref[pl.ds(pl.multiple_of(tile * TILE, TILE), TILE), :]
        here = jnp.dot(order, raw, preferred_element_type=jnp.float32).astype(jnp.bfloat16)
        rows_ref[span, :] = here
        cols_ref[:, span] = lax.dot_general(
            spread, here, (((1,), (1,)), ((), ())), preferred_element_type=jnp.float32
        ).astype(jnp.bfloat16)
    fetch.wait()
    for pair in range(4):
        span = slice(pair * 2 * TILE, (pair + 1) * 2 * TILE)
        for section in range(sections):
            cut = slice(section * quarter, (section + 1) * quarter)
            scores = lax.dot_general(
                rows_ref[span, :], halved_ref[cut, :], (((1,), (1,)), ((), ())), preferred_element_type=jnp.float32
            )
            for sub in range(2):
                tile = tiles[pair * 2 + sub]
                words = words_ref[section, pl.ds(pl.multiple_of(tile * WORDS, WORDS), WORDS), :]
                for plane in range(PLANES):
                    at = sub * TILE + plane * WORDS
                    sign = jnp.where((words & (1 << plane)) == 0, 1.0, -1.0)
                    error = jnp.tanh(scores[at : at + WORDS, :]) + sign
                    error_ref[pair * 2 * TILE + at : pair * 2 * TILE + at + WORDS, cut] = error.astype(jnp.bfloat16)
        row = jnp.dot(error_ref[span, :], block_ref[...], preferred_element_type=jnp.float32)
        store = keep_ref if pair // 2 else send_ref
        store[pair % 2] = row
    for section in range(sections):
        cut = slice(section * quarter, (section + 1) * quarter)
        col_ref[:, cut] = jnp.dot(cols_ref[...], error_ref[:, cut], preferred_element_type=jnp.float32)


def to_line_sum_kernel(came_ref, out_ref):
    total = came_ref[0]
    for part in range(1, came_ref.shape[0]):
        total = total + came_ref[part]
    deep = out_ref.shape[1]
    for part in range(out_ref.shape[0]):
        out_ref[part] = total[part * deep : (part + 1) * deep, :]


def to_owner_kernel(owners_ref, came_ref, out_ref):
    total = came_ref[0]
    for part in range(1, came_ref.shape[0]):
        total = total + came_ref[part]
    out_ref[...] = jnp.zeros_like(out_ref)
    quarter = out_ref.shape[2]
    for s in range(SECTIONS):
        out_ref[owners_ref[s]] = total[:, s * quarter : (s + 1) * quarter]


def finish_kernel(scale, owners_ref, keep_ref, came_ref, back_ref, out_ref, row_ref):
    mine = lax.axis_index("blk")
    owned = jnp.bool_(False)
    for s in range(SECTIONS):
        owned = owned | (owners_ref[s] == mine)
    quarter, width = out_ref.shape
    blocks, deep, _ = back_ref.shape
    row = keep_ref[0] + came_ref[...].astype(jnp.float32)
    for tile in range(quarter // TILE):
        for plane in range(PLANES):
            at = tile * TILE + plane * WORDS
            for lane in range(width // 128):
                row_ref[lane, pl.ds(tile * TILE + plane, WORDS, stride=PLANES), :] = row[
                    at : at + WORDS, lane * 128 : (lane + 1) * 128
                ]
    for lane in range(width // 128):
        out_ref[:, lane * 128 : (lane + 1) * 128] = row_ref[lane] * scale

    @pl.when(owned)
    def _():
        col = back_ref[...].reshape(blocks * deep, quarter)
        out_ref[...] += col.T * scale


def body(embedding, adjacency, owners):
    rows, width = embedding.shape
    sections = adjacency.shape[0]
    groups = lax.axis_size("grp")
    blocks = lax.axis_size("blk")
    quarter = rows // groups
    wide = sections * quarter
    plane_xy = [[x * 32 + z * 4 + y for x in range(2) for y in range(4)] for z in range(LINE)]
    line_z = [[x * 32 + z * 4 + y for z in range(LINE)] for x in range(2) for y in range(4)]

    def swap(value, line=None):
        return lax.all_to_all(value, "blk", 0, 0, axis_index_groups=line)

    def shape(*extent, dtype=jnp.float32):
        return jax.ShapeDtypeStruct(extent, dtype)

    half = jnp.bfloat16
    deep, lanes = 2 * quarter // blocks, width // 2
    own, owners = local_call(
        own_kernel,
        (shape(blocks, deep, lanes, dtype=half), shape(blocks, dtype=jnp.int32)),
        [ANYWHERE, ANYWHERE],
        [pltpu.VMEM((quarter, width), half), pltpu.SemaphoreType.DMA((2,))],
        limit=60,
    )(owners, embedding)
    got = swap(own)
    sent = local_call(to_line_kernel, shape(LINE, sections, deep, lanes, dtype=half), [SCALARS, VECTORS])(owners, got)
    came = swap(sent, line_z)
    spread = local_call(to_plane_kernel, shape(LINE, LINE, sections, deep, lanes, dtype=half), [VECTORS])(came)
    pieces = swap(spread, plane_xy)

    keep, send, col = local_call(
        products_kernel,
        (shape(2, quarter, width), shape(2, quarter, width), shape(width, wide)),
        [VECTORS, VECTORS, ANYWHERE],
        [
            pltpu.VMEM((wide, width), half),
            pltpu.VMEM((wide, width), half),
            pltpu.VMEM((rows, width), half),
            pltpu.VMEM((width, rows), half),
            pltpu.VMEM((rows, wide), half),
            pltpu.VMEM(adjacency.shape, jnp.int32),
            pltpu.SemaphoreType.DMA,
        ],
        pl.CostEstimate(flops=6 * rows * wide * width, bytes_accessed=9 << 20, transcendentals=rows * wide),
        limit=32,
    )(embedding, pieces, adjacency)

    keep = keep + lax.ppermute(send, "grp", [(g, g ^ 1) for g in range(groups)])
    came = lax.ppermute(keep[1].astype(jnp.float16), "grp", [(g, g ^ 2) for g in range(groups)]).astype(jnp.float32)
    col = swap(col.astype(jnp.float16).reshape(LINE, width // LINE, wide), plane_xy).astype(jnp.float32)
    col = local_call(to_line_sum_kernel, shape(LINE, width // blocks, wide), [VECTORS])(col)
    col = swap(col, line_z)
    col = local_call(to_owner_kernel, shape(blocks, width // blocks, quarter), [SCALARS, VECTORS])(owners, col)
    back = swap(col)
    return local_call(
        functools.partial(finish_kernel, 0.5 * rows ** (-0.5)),
        shape(quarter, width),
        [SCALARS, VECTORS, VECTORS, VECTORS],
        [pltpu.VMEM((width // 128, quarter, 128), jnp.float32)],
    )(owners, keep, came, back)


def solution(mesh):
    return jax.shard_map(
        body,
        mesh=mesh,
        in_specs=(P("blk", None), P(None, "blk", "grp"), P()),
        out_specs=P(("blk", "grp"), None),
        check_vma=False,
    )
```

time: 1300 us -> 119 us (0.09)
  waiting for transfers between devices: 1220 us -> 21.2 us
  blocking collectives: 0 us -> 65.9 us
  local copies, waits for them, and re-layouts: 36 us -> 0.77 us
  matrix products: 21 us -> 0 us
  between operations: 15.8 us -> 0.11 us
  Pallas kernels: 0 us -> 13.6 us
    psum x2 -> x0, waiting for transfers between devices: 1170 us -> none  [the longest x1 600 us: body(): summed = lax.psum(column, 'blk')]
    all_to_all x0 -> x4, blocking collectives: none -> 65.9 us  [swap(): return lax.all_to_all(value, 'blk', 0, 0, axis_index_groups=line)]
    reduce_scatter x1 -> x0, waiting for transfers between devices: 47.1 us -> none  [body(): lax.psum_scatter(row_total, 'grp', scatter_dimension=0, tiled=True)]
    shift_right_arithmetic x9 -> x0, local copies, waits for them, and re-layouts: 32.1 us -> none  [body(): jnp.right_shift(words[:, None, :], shifts[None, :, None]) & 1]
    dot_general x12 -> x0, matrix products: 21 us -> none  [the longest x4 8.73 us: body(): jnp.einsum('rw,cw->rc', embedding, block, preferred_element_type=jnp.floa...]
    all_to_all x0 -> x2, waiting for transfers between devices: none -> 14 us  [swap(): return lax.all_to_all(value, 'blk', 0, 0, axis_index_groups=line)]
    pallas_call x0 -> x7, Pallas kernels: none -> 13.6 us  [the longest x1 8.19 us: body(): local_call(products_kernel, (shape(2, quarter, width), shape(2, quarter,...]
  transfers between devices with their start and end apart: 3 -> 4, of which waited for: 3 -> 3; matrix products, arithmetic and copies ran while one was open for 3% -> 2% of each run, Pallas kernels for 0% -> 1%
where the time goes in v2:
time: 119 us; the launch traced here: 118 us
  blocking collectives  65.9 us (55%)
  waiting for transfers between devices  21.2 us (18%)
  Pallas kernels  13.6 us (11%)
  starting transfers between devices  12.9 us (11%)
  other arithmetic  3.96 us (3%)
    all_to_all x4, blocking collectives, swap(): return lax.all_to_all(value, 'blk', 0, 0, axis_index_groups=line)  65.9 us
    all_to_all x2, waiting for transfers between devices, swap(): return lax.all_to_all(value, 'blk', 0, 0, axis_index_groups=line)  14 us
    all_to_all x2, starting transfers between devices, swap(): return lax.all_to_all(value, 'blk', 0, 0, axis_index_groups=line)  10 us
    pallas_call x1, Pallas kernels, body(): local_call(products_kernel, (shape(2, quarter, width), shape(2, quarter,...  8.19 us
    ppermute x1, waiting for transfers between devices, body(): lax.ppermute(keep[1].astype(jnp.float16), 'grp', [(g, g ^ 2) for g in ran...  7.23 us
    ppermute x1, starting transfers between devices, body(): lax.ppermute(keep[1].astype(jnp.float16), 'grp', [(g, g ^ 2) for g in ran...  2.82 us
  transfers between devices with their start and end apart: 4, of which 3 were waited for; matrix products, arithmetic and copies ran while one was open for 2% of the time, Pallas kernels for 1%

profile of v2, /device:TPU:32, one launch (start us, length us, event | category | flops | bytes accessed | tf_op | source)
XLA Modules:
  0.0 118.5 jit_solution(9137869004575280470)
XLA Ops:
  0.0 1.7 %shard_map.37 = (bf16[64,16,128]{2,1,0:T(8,128)(2,1)}, s32[64]{0:T(128)}) custom-call(s32[64]{0:T(128)} %owners_ref.1, bf16[2048,256]{1,0:T(8,128)(2,1)} %emb_ref.3), custom_call_target="tpu_custom_call" | custom-call | tf_op jit(solution)/shard_map/pallas_call | solution.py:191
  1.7 25.8 %all_to_all.30.got_ref = bf16[64,16,128]{2,1,0:T(8,128)(2,1)S(1)} all-to-all(bf16[64,16,128]{2,1,0:T(8,128)(2,1)} %get-tuple-element.11), channel_id=1, replica_groups=mesh['blk'=64,'grp'=4] {'blk'}, dimensions={0} | all-to-all | bytes 524288 | tf_op jit(solution)/shard_map/all_to_all | solution.py:184
  27.5 0.0 copy-start
  27.5 0.0 copy-start.1
  27.5 0.8 copy-done.1
  28.3 0.0 copy-start.3
  28.3 0.6 shard_map.38
  28.9 11.2 %all_to_all.31.came_ref = bf16[8,4,16,128]{3,2,1,0:T(8,128)(2,1)S(1)} all-to-all(bf16[8,4,16,128]{3,2,1,0:T(8,128)(2,1)S(1)} %shard_map.38), channel_id=1, replica_groups={{0,16,32,48,64,80,96,112},{4,20,36,52,68,84,100,116},{8,24,40,56,72,88,..., dimensions={0} | all-to-all | bytes 262144 | tf_op jit(solution)/shard_map/all_to_all | solution.py:184
  40.1 0.1 shard_map.39
  40.2 16.0 %all_to_all.32.pieces_ref = bf16[8,8,4,16,128]{4,3,2,1,0:T(8,128)(2,1)S(1)} all-to-all(bf16[8,8,4,16,128]{4,3,2,1,0:T(8,128)(2,1)S(1)} %shard_map.39), channel_id=1, replica_groups={{0,4,8,12,128,132,136,140},{16,20,24,28,144,148,152,156},{32,36,40,44,1..., dimensions={0} | all-to-all | bytes 2097152 | tf_op jit(solution)/shard_map/all_to_all | solution.py:184
  56.2 0.0 copy-done
  56.2 0.0 copy-done.3
  56.2 8.2 %shard_map.40 = (f32[2,512,256]{2,1,0:T(8,128)S(1)}, f32[2,512,256]{2,1,0:T(8,128)S(1)}, f32[256,2048]{1,0:T(8,128)S(1)}) custom-call(bf16[2048,256]{1,0:T(8,128)(2,1)S(1)} %copy-done, bf16[8,8,4,16,128]{4,3,2,1,0:T(8,128)(2,1)S(1)} %all_to_all.32.pieces_ref, s32[4,256,512]{2,1,0:T(8,128)S(1)} %copy-done.3), custom_call_target="tpu_custom_call" | custom-call | flops 6442450944 | bytes 9437184 | tf_op jit(solution)/shard_map/pallas_call | solution.py:204
  64.4 1.1 convert_element_type.15
  65.6 4.2 %all-to-all-start.3 = ((f16[8,32,2048]{2,1,0:T(8,128)(2,1)}), f16[8,32,2048]{2,1,0:T(8,128)(2,1)}, u32[]{:S(2)}, u32[]{:S(2)}) async-start(f16[8,32,2048]{2,1,0:T(8,128)(2,1)} %bitcast.1), calls=%async_computation.3 | async-start | bytes 2097152 | tf_op jit(solution)/shard_map/all_to_all | solution.py:184
  69.8 0.1 collective-permute-start
  69.9 10.6 %all-to-all-done.3 = f16[8,32,2048]{2,1,0:T(8,128)(2,1)} async-done(((f16[8,32,2048]{2,1,0:T(8,128)(2,1)}), f16[8,32,2048]{2,1,0:T(8,128)(2,1)}, u32[]{:S(2)}, u32[]{:S(2)}) %all-to-all-start.3) | async-done | bytes 1048608 | tf_op jit(solution)/shard_map/all_to_all | solution.py:184
  80.5 1.4 %convert_element_type.16.came_ref = f32[8,32,2048]{2,1,0:T(8,128)S(1)} convert(f16[8,32,2048]{2,1,0:T(8,128)(2,1)} %all-to-all-done.3) | non-fusion elementwise | flops 524288 | bytes 3145728 | tf_op jit(solution)/shard_map/convert_element_type | solution.py:223
  81.9 0.0 copy-start.2
  81.9 0.1 shard_map.41
  82.0 12.9 %all_to_all.33.came_ref = f32[8,4,2048]{2,1,0:T(4,128)S(1)} all-to-all(f32[8,4,2048]{2,1,0:T(4,128)S(1)} %shard_map.41), channel_id=1, replica_groups={{0,16,32,48,64,80,96,112},{4,20,36,52,68,84,100,116},{8,24,40,56,72,88,..., dimensions={0} | all-to-all | bytes 524288 | tf_op jit(solution)/shard_map/all_to_all | solution.py:184
  94.9 0.0 copy-done.2
  94.9 1.4 %shard_map.42 = f32[64,4,512]{2,1,0:T(4,128)} custom-call(s32[64]{0:T(128)S(1)} %copy-done.2, f32[8,4,2048]{2,1,0:T(4,128)S(1)} %all_to_all.33.came_ref), custom_call_target="tpu_custom_call" | custom-call | tf_op jit(solution)/shard_map/pallas_call | solution.py:226
  96.3 5.8 %all-to-all-start.5 = ((f32[64,4,512]{2,1,0:T(4,128)}), f32[64,4,512]{2,1,0:T(4,128)S(1)}, u32[]{:S(2)}, u32[]{:S(2)}) async-start(f32[64,4,512]{2,1,0:T(4,128)} %shard_map.42), calls=%async_computation.5 | async-start | bytes 1048576 | tf_op jit(solution)/shard_map/all_to_all | solution.py:184
  102.1 0.0 collective-permute-done
  102.1 1.4 %add.3.keep_ref = f32[2,512,256]{2,1,0:T(8,128)S(1)} add(f32[2,512,256]{2,1,0:T(8,128)S(1)} %get-tuple-element.12, f32[2,512,256]{2,1,0:T(8,128)} %collective-permute-done) | non-fusion elementwise | flops 262144 | bytes 3145728 | tf_op jit(solution)/shard_map/add | solution.py:221
  103.5 2.8 %collective-permute-start.1 = (f16[512,256]{1,0:T(8,128)(2,1)S(1)}, f16[512,256]{1,0:T(8,128)(2,1)S(1)}, u32[]{:S(2)}, u32[]{:S(2)}) collective-permute-start(f16[512,256]{1,0:T(8,128)(2,1)S(1)} %fusion), channel_id=1, source_target_pairs={{0,2},{1,3},{2,0},{3,1},{4,6},{5,7},{6,4},{7,5},{8,10},{9,11},{10,... | collective-permute-start | bytes 786440 | tf_op jit(solution)/shard_map/ppermute | solution.py:222
  106.3 7.2 %collective-permute-done.1 = f16[512,256]{1,0:T(8,128)(2,1)S(1)} collective-permute-done((f16[512,256]{1,0:T(8,128)(2,1)S(1)}, f16[512,256]{1,0:T(8,128)(2,1)S(1)}, u32[]{:S(2)}, u32[]{:S(2)}) %collective-permute-start.1) | collective-permute-done | bytes 262176 | tf_op jit(solution)/shard_map/ppermute | solution.py:222
  113.6 3.4 %all-to-all-done.5.back_ref = f32[64,4,512]{2,1,0:T(4,128)S(1)} async-done(((f32[64,4,512]{2,1,0:T(4,128)}), f32[64,4,512]{2,1,0:T(4,128)S(1)}, u32[]{:S(2)}, u32[]{:S(2)}) %all-to-all-start.5) | async-done | bytes 524320 | tf_op jit(solution)/shard_map/all_to_all | solution.py:184
  117.0 1.5 %shard_map.43 = f32[512,256]{1,0:T(8,128)} custom-call(s32[64]{0:T(128)S(1)} %copy-done.2, f32[2,512,256]{2,1,0:T(8,128)S(1)} %add.3.keep_ref, f32[512,256]{1,0:T(8,128)S(1)} %convert_element_type.14.came_ref, f32[64,4,512]{2,1,0:T(4,128)S(1)} %all-to-all-done.5.back_ref), custom_call_target="tpu_custom_call" | custom-call | tf_op jit(solution)/shard_map/pallas_call | solution.py:228
  (2 shorter events, 0.1 us)
Async XLA Ops:
  27.5 28.7 %copy-start = (bf16[2048,256]{1,0:T(8,128)(2,1)S(1)}, bf16[2048,256]{1,0:T(8,128)(2,1)}, u32[]{:S(2)}) copy-start(bf16[2048,256]{1,0:T(8,128)(2,1)} %emb_ref.3) | copy-start | bytes 3145732
  27.5 0.8 copy-start.1
  28.3 27.9 %copy-start.3 = (s32[4,256,512]{2,1,0:T(8,128)S(1)}, s32[4,256,512]{2,1,0:T(8,128)}, u32[]{:S(2)}) copy-start(s32[4,256,512]{2,1,0:T(8,128)} %far_words_ref.1) | copy-start | bytes 6291460
  65.6 14.9 %all-to-all-start.3 = ((f16[8,32,2048]{2,1,0:T(8,128)(2,1)}), f16[8,32,2048]{2,1,0:T(8,128)(2,1)}, u32[]{:S(2)}, u32[]{:S(2)}) async-start(f16[8,32,2048]{2,1,0:T(8,128)(2,1)} %bitcast.1), calls=%async_computation.3 | async-start | bytes 2097152 | tf_op jit(solution)/shard_map/all_to_all | solution.py:184
  69.8 32.3 %collective-permute-start = (f32[2,512,256]{2,1,0:T(8,128)S(1)}, f32[2,512,256]{2,1,0:T(8,128)}, u32[]{:S(2)}, u32[]{:S(2)}) collective-permute-start(f32[2,512,256]{2,1,0:T(8,128)S(1)} %get-tuple-element.13), channel_id=1, source_target_pairs={{0,1},{1,0},{2,3},{3,2},{4,5},{5,4},{6,7},{7,6},{8,9},{9,8},{10,11... | collective-permute-start | bytes 3145736 | tf_op jit(solution)/shard_map/ppermute | solution.py:221
  81.9 13.0 %copy-start.2 = (s32[64]{0:T(128)S(1)}, s32[64]{0:T(128)}, u32[]{:S(2)}) copy-start(s32[64]{0:T(128)} %get-tuple-element.10.owners_ref) | copy-start | bytes 772
  96.3 20.7 %all-to-all-start.5 = ((f32[64,4,512]{2,1,0:T(4,128)}), f32[64,4,512]{2,1,0:T(4,128)S(1)}, u32[]{:S(2)}, u32[]{:S(2)}) async-start(f32[64,4,512]{2,1,0:T(4,128)} %shard_map.42), calls=%async_computation.5 | async-start | bytes 1048576 | tf_op jit(solution)/shard_map/all_to_all | solution.py:184
  103.5 10.0 %collective-permute-start.1 = (f16[512,256]{1,0:T(8,128)(2,1)S(1)}, f16[512,256]{1,0:T(8,128)(2,1)S(1)}, u32[]{:S(2)}, u32[]{:S(2)}) collective-permute-start(f16[512,256]{1,0:T(8,128)(2,1)S(1)} %fusion), channel_id=1, source_target_pairs={{0,2},{1,3},{2,0},{3,1},{4,6},{5,7},{6,4},{7,5},{8,10},{9,11},{10,... | collective-permute-start | bytes 786440 | tf_op jit(solution)/shard_map/ppermute | solution.py:222

commit v3 on v2

--- a/solution.py
+++ b/solution.py
@@ -18,7 +18,7 @@
 VECTORS = pl.BlockSpec(memory_space=pltpu.VMEM)
 
 
-def local_call(kernel, outs, ins, scratch=(), cost=None, limit=32):
+def local_call(kernel, outs, ins, scratch=(), cost=None, limit=32 << 20):
     return pl.pallas_call(
         kernel,
         out_shape=outs,
@@ -26,7 +26,7 @@
         out_specs=jax.tree.map(lambda _: VECTORS, outs),
         scratch_shapes=scratch,
         cost_estimate=cost,
-        compiler_params=pltpu.CompilerParams(vmem_limit_bytes=limit << 20),
+        compiler_params=pltpu.CompilerParams(vmem_limit_bytes=limit),
     )
 
 
@@ -94,7 +94,7 @@
     for away in (1, 0):
         for other in (0, 1):
             for sub in range(2):
-                tiles.append(((high ^ other) * 2 + (core ^ away)) * 2 + sub)
+                tiles.append(((high ^ away) * 2 + (core ^ other)) * 2 + sub)
     for step, tile in enumerate(tiles):
         span = slice(step * TILE, (step + 1) * TILE)
         raw = emb_ref[pl.ds(pl.multiple_of(tile * TILE, TILE), TILE), :]
@@ -127,23 +127,26 @@
         col_ref[:, cut] = jnp.dot(cols_ref[...], error_ref[:, cut], preferred_element_type=jnp.float32)
 
 
-def to_line_sum_kernel(came_ref, out_ref):
+def plane_total(came_ref):
     total = came_ref[0]
     for part in range(1, came_ref.shape[0]):
         total = total + came_ref[part]
+    return total
+
+
+def to_line_sum_kernel(came_ref, out_ref):
+    total = plane_total(came_ref)
     deep = out_ref.shape[1]
     for part in range(out_ref.shape[0]):
         out_ref[part] = total[part * deep : (part + 1) * deep, :]
 
 
 def to_owner_kernel(owners_ref, came_ref, out_ref):
-    total = came_ref[0]
-    for part in range(1, came_ref.shape[0]):
-        total = total + came_ref[part]
+    total = plane_total(came_ref)
     out_ref[...] = jnp.zeros_like(out_ref)
     quarter = out_ref.shape[2]
     for s in range(SECTIONS):
-        out_ref[owners_ref[s]] = total[:, s * quarter : (s + 1) * quarter]
+        out_ref[owners_ref[s]] = total[:, s * quarter : (s + 1) * quarter] * 0.125
 
 
 def finish_kernel(scale, owners_ref, keep_ref, came_ref, back_ref, out_ref, row_ref):
@@ -152,7 +155,6 @@
     for s in range(SECTIONS):
         owned = owned | (owners_ref[s] == mine)
     quarter, width = out_ref.shape
-    blocks, deep, _ = back_ref.shape
     row = keep_ref[0] + came_ref[...].astype(jnp.float32)
     for tile in range(quarter // TILE):
         for plane in range(PLANES):
@@ -166,8 +168,7 @@
 
     @pl.when(owned)
     def _():
-        col = back_ref[...].reshape(blocks * deep, quarter)
-        out_ref[...] += col.T * scale
+        out_ref[...] += back_ref[...].reshape(width, quarter).T * (8.0 * scale)
 
 
 def body(embedding, adjacency, owners):
@@ -180,6 +181,8 @@
     plane_xy = [[x * 32 + z * 4 + y for x in range(2) for y in range(4)] for z in range(LINE)]
     line_z = [[x * 32 + z * 4 + y for z in range(LINE)] for x in range(2) for y in range(4)]
 
+    fence = lax.optimization_barrier
+
     def swap(value, line=None):
         return lax.all_to_all(value, "blk", 0, 0, axis_index_groups=line)
 
@@ -193,7 +196,6 @@
         (shape(blocks, deep, lanes, dtype=half), shape(blocks, dtype=jnp.int32)),
         [ANYWHERE, ANYWHERE],
         [pltpu.VMEM((quarter, width), half), pltpu.SemaphoreType.DMA((2,))],
-        limit=60,
     )(owners, embedding)
     got = swap(own)
     sent = local_call(to_line_kernel, shape(LINE, sections, deep, lanes, dtype=half), [SCALARS, VECTORS])(owners, got)
@@ -215,22 +217,25 @@
             pltpu.SemaphoreType.DMA,
         ],
         pl.CostEstimate(flops=6 * rows * wide * width, bytes_accessed=9 << 20, transcendentals=rows * wide),
-        limit=32,
     )(embedding, pieces, adjacency)
 
-    keep = keep + lax.ppermute(send, "grp", [(g, g ^ 1) for g in range(groups)])
-    came = lax.ppermute(keep[1].astype(jnp.float16), "grp", [(g, g ^ 2) for g in range(groups)]).astype(jnp.float32)
-    col = swap(col.astype(jnp.float16).reshape(LINE, width // LINE, wide), plane_xy).astype(jnp.float32)
+    col = col.astype(jnp.float16).reshape(LINE, width // LINE, wide)
+    col = fence(swap(fence(col), plane_xy))
+    col, keep, send = fence((col.astype(jnp.float32), keep, send))
     col = local_call(to_line_sum_kernel, shape(LINE, width // blocks, wide), [VECTORS])(col)
-    col = swap(col, line_z)
+    far = lax.ppermute(send.astype(jnp.float16), "grp", [(g, g ^ 2) for g in range(groups)])
+    col = swap(col.astype(jnp.float16), line_z).astype(jnp.float32)
+    col, far, keep = fence((col, far, keep))
+    keep = keep + far.astype(jnp.float32)
     col = local_call(to_owner_kernel, shape(blocks, width // blocks, quarter), [SCALARS, VECTORS])(owners, col)
-    back = swap(col)
+    far = lax.ppermute(keep[1].astype(jnp.float16), "grp", [(g, g ^ 1) for g in range(groups)]).astype(jnp.float32)
+    back = swap(col.astype(jnp.float16)).astype(jnp.float32)
     return local_call(
         functools.partial(finish_kernel, 0.5 * rows ** (-0.5)),
         shape(quarter, width),
         [SCALARS, VECTORS, VECTORS, VECTORS],
         [pltpu.VMEM((width // 128, quarter, 128), jnp.float32)],
-    )(owners, keep, came, back)
+    )(owners, keep, far, back)
 
 
 def solution(mesh):

time: 119 us -> 115 us (0.966)
  blocking collectives: 65.9 us -> 79.4 us
  waiting for transfers between devices: 21.2 us -> 11.4 us
  starting transfers between devices: 12.9 us -> 8.65 us
  Pallas kernels: 13.6 us -> 11.1 us
  other arithmetic: 3.96 us -> 1.61 us
    all_to_all x4 -> x5, blocking collectives: 65.9 us -> 79.4 us  [swap(): return lax.all_to_all(value, 'blk', 0, 0, axis_index_groups=line)]
    ppermute x2, waiting for transfers between devices: 7.23 us -> 1.52 us  [the longest x1 1.52 us: body(): lax.ppermute(keep[1].astype(jnp.float16), 'grp', [(g, g ^ 1) for g in ran...]
    all_to_all x2 -> x1, starting transfers between devices: 10 us -> 5.54 us  [swap(): return lax.all_to_all(value, 'blk', 0, 0, axis_index_groups=line)]
    all_to_all x2 -> x1, waiting for transfers between devices: 14 us -> 9.92 us  [swap(): return lax.all_to_all(value, 'blk', 0, 0, axis_index_groups=line)]
    pallas_call x1, Pallas kernels: 1.72 us -> 0.09 us  [body(): local_call(own_kernel, (shape(blocks, deep, lanes, dtype=half), shape(blo...]
    add x1, other arithmetic: 1.36 us -> 0.16 us  [body(): keep = keep + far.astype(jnp.float32)]
    convert_element_type x3 -> x8, other arithmetic: 2.56 us -> 1.4 us  [the longest x2 0.89 us: body(): back = swap(col.astype(jnp.float16)).astype(jnp.float32)]
  transfers between devices with their start and end apart: 4 -> 3, of which waited for: 3 -> 2; matrix products, arithmetic and copies ran while one was open for 2% -> 0% of each run, Pallas kernels for 1% -> 0%
where the time goes in v3:
time: 115 us; the launch traced here: 114 us
  blocking collectives  79.4 us (69%)
  waiting for transfers between devices  11.4 us (10%)
  Pallas kernels  11.1 us (10%)
  starting transfers between devices  8.65 us (8%)
  local copies, waits for them, and re-layouts  1.89 us (2%)
  other arithmetic  1.61 us (1%)
    all_to_all x5, blocking collectives, swap(): return lax.all_to_all(value, 'blk', 0, 0, axis_index_groups=line)  79.4 us
    all_to_all x1, waiting for transfers between devices, swap(): return lax.all_to_all(value, 'blk', 0, 0, axis_index_groups=line)  9.92 us
    pallas_call x1, Pallas kernels, body(): local_call(products_kernel, (shape(2, quarter, width), shape(2, quarter,...  8.16 us
    all_to_all x1, starting transfers between devices, swap(): return lax.all_to_all(value, 'blk', 0, 0, axis_index_groups=line)  5.54 us
    ppermute x1, starting transfers between devices, body(): lax.ppermute(send.astype(jnp.float16), 'grp', [(g, g ^ 2) for g in range(...  3.02 us
  transfers between devices with their start and end apart: 3, of which 2 were waited for; matrix products, arithmetic and copies ran while one was open for 0% of the time, Pallas kernels for 0%

profile of v3, /device:TPU:32, one launch (start us, length us, event | category | flops | bytes accessed | tf_op | source)
XLA Modules:
  0.0 114.3 jit_solution(8303978276074046830)
XLA Ops:
  0.0 0.0 copy-start
  0.0 1.2 %copy-done = bf16[2048,256]{1,0:T(8,128)(2,1)S(1)} copy-done((bf16[2048,256]{1,0:T(8,128)(2,1)S(1)}, bf16[2048,256]{1,0:T(8,128)(2,1)}, u32[]{:S(2)}) %copy-start) | copy-done | bytes 1048600
  1.2 0.0 copy-start.2
  1.2 0.7 copy-done.2
  1.9 0.1 shard_map.37
  2.0 25.6 %all_to_all.30.got_ref = bf16[64,16,128]{2,1,0:T(8,128)(2,1)S(1)} all-to-all(bf16[64,16,128]{2,1,0:T(8,128)(2,1)S(1)} %get-tuple-element.17), channel_id=1, replica_groups=mesh['blk'=64,'grp'=4] {'blk'}, dimensions={0} | all-to-all | bytes 524288 | tf_op jit(solution)/shard_map/all_to_all | solution.py:187
  27.6 0.0 copy-start.1
  27.6 0.0 copy-start.3
  27.6 0.6 shard_map.38
  28.1 11.2 %all_to_all.31.came_ref = bf16[8,4,16,128]{3,2,1,0:T(8,128)(2,1)S(1)} all-to-all(bf16[8,4,16,128]{3,2,1,0:T(8,128)(2,1)S(1)} %shard_map.38), channel_id=1, replica_groups={{0,16,32,48,64,80,96,112},{4,20,36,52,68,84,100,116},{8,24,40,56,72,88,..., dimensions={0} | all-to-all | bytes 262144 | tf_op jit(solution)/shard_map/all_to_all | solution.py:187
  39.4 0.1 shard_map.39
  39.5 16.0 %all_to_all.32.pieces_ref = bf16[8,8,4,16,128]{4,3,2,1,0:T(8,128)(2,1)S(1)} all-to-all(bf16[8,8,4,16,128]{4,3,2,1,0:T(8,128)(2,1)S(1)} %shard_map.39), channel_id=1, replica_groups={{0,4,8,12,128,132,136,140},{16,20,24,28,144,148,152,156},{32,36,40,44,1..., dimensions={0} | all-to-all | bytes 2097152 | tf_op jit(solution)/shard_map/all_to_all | solution.py:187
  55.5 0.0 copy-done.1
  55.5 0.0 copy-done.3
  55.5 8.2 %shard_map.40 = (f32[2,512,256]{2,1,0:T(8,128)S(1)}, f32[2,512,256]{2,1,0:T(8,128)S(1)}, f32[256,2048]{1,0:T(8,128)S(1)}) custom-call(bf16[2048,256]{1,0:T(8,128)(2,1)S(1)} %copy-done.1, bf16[8,8,4,16,128]{4,3,2,1,0:T(8,128)(2,1)S(1)} %all_to_all.32.pieces_ref, s32[4,256,512]{2,1,0:T(8,128)S(1)} %copy-done.3), custom_call_target="tpu_custom_call" | custom-call | flops 6442450944 | bytes 9437184 | tf_op jit(solution)/shard_map/pallas_call | solution.py:206
  63.7 0.1 convert_element_type.31
  63.8 15.1 %all_to_all.33 = f16[8,32,2048]{2,1,0:T(8,128)(2,1)S(1)} all-to-all(f16[8,32,2048]{2,1,0:T(8,128)(2,1)S(1)} %bitcast.3), channel_id=1, replica_groups={{0,4,8,12,128,132,136,140},{16,20,24,28,144,148,152,156},{32,36,40,44,1..., dimensions={0} | all-to-all | bytes 2097152 | tf_op jit(solution)/shard_map/all_to_all | solution.py:187
  79.0 0.2 convert_element_type.32.came_ref
  79.1 0.1 convert_element_type.35
  79.2 3.0 %collective-permute-start = (f16[2,512,256]{2,1,0:T(8,128)(2,1)S(1)}, f16[2,512,256]{2,1,0:T(8,128)(2,1)S(1)}, u32[]{:S(2)}, u32[]{:S(2)}) collective-permute-start(f16[2,512,256]{2,1,0:T(8,128)(2,1)S(1)} %convert_element_type.35), channel_id=1, source_target_pairs={{0,2},{1,3},{2,0},{3,1},{4,6},{5,7},{6,4},{7,5},{8,10},{9,11},{10,... | collective-permute-start | bytes 1572872 | tf_op jit(solution)/shard_map/ppermute | solution.py:226
  82.2 0.1 shard_map.41
  82.4 11.5 %all_to_all.34 = f16[8,4,2048]{2,1,0:T(4,128)(2,1)S(1)} all-to-all(f16[8,4,2048]{2,1,0:T(4,128)(2,1)S(1)} %convert_element_type.33), channel_id=1, replica_groups={{0,16,32,48,64,80,96,112},{4,20,36,52,68,84,100,116},{8,24,40,56,72,88,..., dimensions={0} | all-to-all | bytes 262144 | tf_op jit(solution)/shard_map/all_to_all | solution.py:187
  93.9 0.0 collective-permute-done
  93.9 0.6 shard_map.42
  94.5 0.8 convert_element_type.39
  95.3 5.5 %all-to-all-start.5 = ((f16[64,4,512]{2,1,0:T(4,128)(2,1)}), f16[64,4,512]{2,1,0:T(4,128)(2,1)S(1)}, u32[]{:S(2)}, u32[]{:S(2)}) async-start(f16[64,4,512]{2,1,0:T(4,128)(2,1)} %convert_element_type.39), calls=%async_computation.5 | async-start | bytes 524288 | tf_op jit(solution)/shard_map/all_to_all | solution.py:187
  100.9 0.2 convert_add_fusion.keep_ref
  101.1 0.1 collective-permute-start.1
  101.2 1.5 %collective-permute-done.1 = f16[512,256]{1,0:T(8,128)(2,1)S(1)} collective-permute-done((f16[512,256]{1,0:T(8,128)(2,1)S(1)}, f16[512,256]{1,0:T(8,128)(2,1)S(1)}, u32[]{:S(2)}, u32[]{:S(2)}) %collective-permute-start.1) | collective-permute-done | bytes 262176 | tf_op jit(solution)/shard_map/ppermute | solution.py:231
  102.7 9.9 %all-to-all-done.5 = f16[64,4,512]{2,1,0:T(4,128)(2,1)S(1)} async-done(((f16[64,4,512]{2,1,0:T(4,128)(2,1)}), f16[64,4,512]{2,1,0:T(4,128)(2,1)S(1)}, u32[]{:S(2)}, u32[]{:S(2)}) %all-to-all-start.5) | async-done | bytes 262176 | tf_op jit(solution)/shard_map/all_to_all | solution.py:187
  112.7 0.1 convert_element_type.40.back_ref
  112.8 1.5 %shard_map.43 = f32[512,256]{1,0:T(8,128)} custom-call(s32[64]{0:T(128)S(1)} %get-tuple-element.16.owners_ref, f32[2,512,256]{2,1,0:T(8,128)S(1)} %convert_add_fusion.keep_ref, f32[512,256]{1,0:T(8,128)S(1)} %convert_element_type.38.came_ref, f32[64,4,512]{2,1,0:T(4,128)S(1)} %convert_element_type.40.back_ref), custom_call_target="tpu_custom_call" | custom-call | tf_op jit(solution)/shard_map/pallas_call | solution.py:233
  (4 shorter events, 0.2 us)
Async XLA Ops:
  0.0 1.2 %copy-start = (bf16[2048,256]{1,0:T(8,128)(2,1)S(1)}, bf16[2048,256]{1,0:T(8,128)(2,1)}, u32[]{:S(2)}) copy-start(bf16[2048,256]{1,0:T(8,128)(2,1)} %emb_ref.3) | copy-start | bytes 3145732
  1.2 0.7 copy-start.2
  27.6 27.9 %copy-start.1 = (bf16[2048,256]{1,0:T(8,128)(2,1)S(1)}, bf16[2048,256]{1,0:T(8,128)(2,1)}, u32[]{:S(2)}) copy-start(bf16[2048,256]{1,0:T(8,128)(2,1)} %emb_ref.3) | copy-start | bytes 3145732
  27.6 27.9 %copy-start.3 = (s32[4,256,512]{2,1,0:T(8,128)S(1)}, s32[4,256,512]{2,1,0:T(8,128)}, u32[]{:S(2)}) copy-start(s32[4,256,512]{2,1,0:T(8,128)} %far_words_ref.1) | copy-start | bytes 6291460
  79.2 14.7 %collective-permute-start = (f16[2,512,256]{2,1,0:T(8,128)(2,1)S(1)}, f16[2,512,256]{2,1,0:T(8,128)(2,1)S(1)}, u32[]{:S(2)}, u32[]{:S(2)}) collective-permute-start(f16[2,512,256]{2,1,0:T(8,128)(2,1)S(1)} %convert_element_type.35), channel_id=1, source_target_pairs={{0,2},{1,3},{2,0},{3,1},{4,6},{5,7},{6,4},{7,5},{8,10},{9,11},{10,... | collective-permute-start | bytes 1572872 | tf_op jit(solution)/shard_map/ppermute | solution.py:226
  95.3 17.3 %all-to-all-start.5 = ((f16[64,4,512]{2,1,0:T(4,128)(2,1)}), f16[64,4,512]{2,1,0:T(4,128)(2,1)S(1)}, u32[]{:S(2)}, u32[]{:S(2)}) async-start(f16[64,4,512]{2,1,0:T(4,128)(2,1)} %convert_element_type.39), calls=%async_computation.5 | async-start | bytes 524288 | tf_op jit(solution)/shard_map/all_to_all | solution.py:187
  101.1 1.6 %collective-permute-start.1 = (f16[512,256]{1,0:T(8,128)(2,1)S(1)}, f16[512,256]{1,0:T(8,128)(2,1)S(1)}, u32[]{:S(2)}, u32[]{:S(2)}) collective-permute-start(f16[512,256]{1,0:T(8,128)(2,1)S(1)} %fusion), channel_id=1, source_target_pairs={{0,1},{1,0},{2,3},{3,2},{4,5},{5,4},{6,7},{7,6},{8,9},{9,8},{10,11... | collective-permute-start | bytes 786440 | tf_op jit(solution)/shard_map/ppermute | solution.py:231

commit v4 on v3

--- a/solution.py
+++ b/solution.py
@@ -63,13 +63,11 @@
 
 
 def products_kernel(
-    emb_ref, pieces_ref, far_words_ref, keep_ref, send_ref, col_ref,
-    block_ref, halved_ref, rows_ref, cols_ref, error_ref, words_ref, sem,
+    emb_ref, pieces_ref, words_ref, keep_ref, send_ref, col_ref,
+    block_ref, rows_ref, cols_ref, error_ref,
 ):
     plane, line, sections, deep, lanes = pieces_ref.shape
     rows, width = emb_ref.shape
-    fetch = pltpu.make_async_copy(far_words_ref, words_ref, sem)
-    fetch.start()
     quarter = rows // 4
     place = lax.axis_index("grp")
     core, high = place % 2, place // 2
@@ -79,16 +77,14 @@
                 at = section * quarter + (z * 4 + xy % 4) * deep
                 span = slice(at, at + deep)
                 cut = slice(xy // 4 * lanes, (xy // 4 + 1) * lanes)
-                value = pieces_ref[xy, z, section]
-                block_ref[span, cut] = value
-                halved_ref[span, cut] = value * jnp.bfloat16(0.5)
+                block_ref[span, cut] = pieces_ref[xy, z, section]
 
     new = lax.broadcasted_iota(jnp.int32, (TILE, TILE), 0)
     old = lax.broadcasted_iota(jnp.int32, (TILE, TILE), 1)
     pick = old == (new % WORDS) * PLANES + new // WORDS
-    order = jnp.where(pick, 1.0, 0.0).astype(jnp.bfloat16)
+    order = jnp.where(pick, 0.5, 0.0).astype(jnp.bfloat16)
     source = (new // 128) * 128 + (new // 4 % 8) * 16 + (new // 32 % 4) * 4 + new % 4
-    spread = jnp.where(old == source, 1.0, 0.0).astype(jnp.bfloat16)
+    spread = jnp.where(old == source, 2.0, 0.0).astype(jnp.bfloat16)
 
     tiles = []
     for away in (1, 0):
@@ -103,13 +99,12 @@
         cols_ref[:, span] = lax.dot_general(
             spread, here, (((1,), (1,)), ((), ())), preferred_element_type=jnp.float32
         ).astype(jnp.bfloat16)
-    fetch.wait()
     for pair in range(4):
         span = slice(pair * 2 * TILE, (pair + 1) * 2 * TILE)
         for section in range(sections):
             cut = slice(section * quarter, (section + 1) * quarter)
             scores = lax.dot_general(
-                rows_ref[span, :], halved_ref[cut, :], (((1,), (1,)), ((), ())), preferred_element_type=jnp.float32
+                rows_ref[span, :], block_ref[cut, :], (((1,), (1,)), ((), ())), preferred_element_type=jnp.float32
             )
             for sub in range(2):
                 tile = tiles[pair * 2 + sub]
@@ -206,15 +201,12 @@
     keep, send, col = local_call(
         products_kernel,
         (shape(2, quarter, width), shape(2, quarter, width), shape(width, wide)),
-        [VECTORS, VECTORS, ANYWHERE],
+        [VECTORS] * 3,
         [
-            pltpu.VMEM((wide, width), half),
             pltpu.VMEM((wide, width), half),
             pltpu.VMEM((rows, width), half),
             pltpu.VMEM((width, rows), half),
             pltpu.VMEM((rows, wide), half),
-            pltpu.VMEM(adjacency.shape, jnp.int32),
-            pltpu.SemaphoreType.DMA,
         ],
         pl.CostEstimate(flops=6 * rows * wide * width, bytes_accessed=9 << 20, transcendentals=rows * wide),
     )(embedding, pieces, adjacency)

time: 115 us -> 114 us (level)
  no operation moved by 1% of the time
where the time goes in v4:
time: 114 us
  blocking collectives  79.4 us (70%)
  waiting for transfers between devices  11.4 us (10%)
  Pallas kernels  10.5 us (9%)
  starting transfers between devices  8.64 us (8%)
  local copies, waits for them, and re-layouts  1.89 us (2%)
  other arithmetic  1.61 us (1%)
    all_to_all x5, blocking collectives, swap(): return lax.all_to_all(value, 'blk', 0, 0, axis_index_groups=line)  79.4 us
    all_to_all x1, waiting for transfers between devices, swap(): return lax.all_to_all(value, 'blk', 0, 0, axis_index_groups=line)  9.92 us
    pallas_call x1, Pallas kernels, body(): local_call(products_kernel, (shape(2, quarter, width), shape(2, quarter,...  7.54 us
    all_to_all x1, starting transfers between devices, swap(): return lax.all_to_all(value, 'blk', 0, 0, axis_index_groups=line)  5.54 us
    ppermute x1, starting transfers between devices, body(): lax.ppermute(send.astype(jnp.float16), 'grp', [(g, g ^ 2) for g in range(...  3.01 us
  transfers between devices with their start and end apart: 3, of which 2 were waited for; matrix products, arithmetic and copies ran while one was open for 0% of the time, Pallas kernels for 0%

profile of v4, /device:TPU:32, one launch (start us, length us, event | category | flops | bytes accessed | tf_op | source)
XLA Modules:
  0.0 113.6 jit_solution(10942987821677152753)
XLA Ops:
  0.0 0.0 copy-start
  0.0 1.2 %copy-done = bf16[2048,256]{1,0:T(8,128)(2,1)S(1)} copy-done((bf16[2048,256]{1,0:T(8,128)(2,1)S(1)}, bf16[2048,256]{1,0:T(8,128)(2,1)}, u32[]{:S(2)}) %copy-start) | copy-done | bytes 1048600
  1.2 0.0 copy-start.2
  1.2 0.7 copy-done.2
  1.9 0.1 shard_map.37
  2.0 25.6 %all_to_all.30.got_ref = bf16[64,16,128]{2,1,0:T(8,128)(2,1)S(1)} all-to-all(bf16[64,16,128]{2,1,0:T(8,128)(2,1)S(1)} %get-tuple-element.17), channel_id=1, replica_groups=mesh['blk'=64,'grp'=4] {'blk'}, dimensions={0} | all-to-all | bytes 524288 | tf_op jit(solution)/shard_map/all_to_all | solution.py:182
  27.6 0.0 copy-start.1
  27.6 0.0 copy-start.3
  27.6 0.6 shard_map.38
  28.1 11.2 %all_to_all.31.came_ref = bf16[8,4,16,128]{3,2,1,0:T(8,128)(2,1)S(1)} all-to-all(bf16[8,4,16,128]{3,2,1,0:T(8,128)(2,1)S(1)} %shard_map.38), channel_id=1, replica_groups={{0,16,32,48,64,80,96,112},{4,20,36,52,68,84,100,116},{8,24,40,56,72,88,..., dimensions={0} | all-to-all | bytes 262144 | tf_op jit(solution)/shard_map/all_to_all | solution.py:182
  39.4 0.1 shard_map.39
  39.5 16.0 %all_to_all.32.pieces_ref = bf16[8,8,4,16,128]{4,3,2,1,0:T(8,128)(2,1)S(1)} all-to-all(bf16[8,8,4,16,128]{4,3,2,1,0:T(8,128)(2,1)S(1)} %shard_map.39), channel_id=1, replica_groups={{0,4,8,12,128,132,136,140},{16,20,24,28,144,148,152,156},{32,36,40,44,1..., dimensions={0} | all-to-all | bytes 2097152 | tf_op jit(solution)/shard_map/all_to_all | solution.py:182
  55.5 0.0 copy-done.1
  55.5 0.0 copy-done.3
  55.5 7.5 %shard_map.40 = (f32[2,512,256]{2,1,0:T(8,128)S(1)}, f32[2,512,256]{2,1,0:T(8,128)S(1)}, f32[256,2048]{1,0:T(8,128)S(1)}) custom-call(bf16[2048,256]{1,0:T(8,128)(2,1)S(1)} %copy-done.1, bf16[8,8,4,16,128]{4,3,2,1,0:T(8,128)(2,1)S(1)} %all_to_all.32.pieces_ref, s32[4,256,512]{2,1,0:T(8,128)S(1)} %copy-done.3), custom_call_target="tpu_custom_call" | custom-call | flops 6442450944 | bytes 9437184 | tf_op jit(solution)/shard_map/pallas_call | solution.py:201
  63.0 0.1 convert_element_type.31
  63.2 15.1 %all_to_all.33 = f16[8,32,2048]{2,1,0:T(8,128)(2,1)S(1)} all-to-all(f16[8,32,2048]{2,1,0:T(8,128)(2,1)S(1)} %bitcast.3), channel_id=1, replica_groups={{0,4,8,12,128,132,136,140},{16,20,24,28,144,148,152,156},{32,36,40,44,1..., dimensions={0} | all-to-all | bytes 2097152 | tf_op jit(solution)/shard_map/all_to_all | solution.py:182
  78.3 0.2 convert_element_type.32.came_ref
  78.5 0.1 convert_element_type.35
  78.6 3.0 %collective-permute-start = (f16[2,512,256]{2,1,0:T(8,128)(2,1)S(1)}, f16[2,512,256]{2,1,0:T(8,128)(2,1)S(1)}, u32[]{:S(2)}, u32[]{:S(2)}) collective-permute-start(f16[2,512,256]{2,1,0:T(8,128)(2,1)S(1)} %convert_element_type.35), channel_id=1, source_target_pairs={{0,2},{1,3},{2,0},{3,1},{4,6},{5,7},{6,4},{7,5},{8,10},{9,11},{10,... | collective-permute-start | bytes 1572872 | tf_op jit(solution)/shard_map/ppermute | solution.py:218
  81.6 0.1 shard_map.41
  81.8 11.5 %all_to_all.34 = f16[8,4,2048]{2,1,0:T(4,128)(2,1)S(1)} all-to-all(f16[8,4,2048]{2,1,0:T(4,128)(2,1)S(1)} %convert_element_type.33), channel_id=1, replica_groups={{0,16,32,48,64,80,96,112},{4,20,36,52,68,84,100,116},{8,24,40,56,72,88,..., dimensions={0} | all-to-all | bytes 262144 | tf_op jit(solution)/shard_map/all_to_all | solution.py:182
  93.3 0.0 collective-permute-done
  93.3 0.6 shard_map.42
  93.9 0.8 convert_element_type.39
  94.7 5.5 %all-to-all-start.5 = ((f16[64,4,512]{2,1,0:T(4,128)(2,1)}), f16[64,4,512]{2,1,0:T(4,128)(2,1)S(1)}, u32[]{:S(2)}, u32[]{:S(2)}) async-start(f16[64,4,512]{2,1,0:T(4,128)(2,1)} %convert_element_type.39), calls=%async_computation.5 | async-start | bytes 524288 | tf_op jit(solution)/shard_map/all_to_all | solution.py:182
  100.2 0.2 convert_add_fusion.keep_ref
  100.5 0.1 collective-permute-start.1
  100.6 1.5 %collective-permute-done.1 = f16[512,256]{1,0:T(8,128)(2,1)S(1)} collective-permute-done((f16[512,256]{1,0:T(8,128)(2,1)S(1)}, f16[512,256]{1,0:T(8,128)(2,1)S(1)}, u32[]{:S(2)}, u32[]{:S(2)}) %collective-permute-start.1) | collective-permute-done | bytes 262176 | tf_op jit(solution)/shard_map/ppermute | solution.py:223
  102.1 9.9 %all-to-all-done.5 = f16[64,4,512]{2,1,0:T(4,128)(2,1)S(1)} async-done(((f16[64,4,512]{2,1,0:T(4,128)(2,1)}), f16[64,4,512]{2,1,0:T(4,128)(2,1)S(1)}, u32[]{:S(2)}, u32[]{:S(2)}) %all-to-all-start.5) | async-done | bytes 262176 | tf_op jit(solution)/shard_map/all_to_all | solution.py:182
  112.0 0.1 convert_element_type.40.back_ref
  112.1 1.5 %shard_map.43 = f32[512,256]{1,0:T(8,128)} custom-call(s32[64]{0:T(128)S(1)} %get-tuple-element.16.owners_ref, f32[2,512,256]{2,1,0:T(8,128)S(1)} %convert_add_fusion.keep_ref, f32[512,256]{1,0:T(8,128)S(1)} %convert_element_type.38.came_ref, f32[64,4,512]{2,1,0:T(4,128)S(1)} %convert_element_type.40.back_ref), custom_call_target="tpu_custom_call" | custom-call | tf_op jit(solution)/shard_map/pallas_call | solution.py:225
  (4 shorter events, 0.2 us)
Async XLA Ops:
  0.0 1.2 %copy-start = (bf16[2048,256]{1,0:T(8,128)(2,1)S(1)}, bf16[2048,256]{1,0:T(8,128)(2,1)}, u32[]{:S(2)}) copy-start(bf16[2048,256]{1,0:T(8,128)(2,1)} %emb_ref.3) | copy-start | bytes 3145732
  1.2 0.7 copy-start.2
  27.6 27.9 %copy-start.1 = (bf16[2048,256]{1,0:T(8,128)(2,1)S(1)}, bf16[2048,256]{1,0:T(8,128)(2,1)}, u32[]{:S(2)}) copy-start(bf16[2048,256]{1,0:T(8,128)(2,1)} %emb_ref.3) | copy-start | bytes 3145732
  27.6 27.9 %copy-start.3 = (s32[4,256,512]{2,1,0:T(8,128)S(1)}, s32[4,256,512]{2,1,0:T(8,128)}, u32[]{:S(2)}) copy-start(s32[4,256,512]{2,1,0:T(8,128)} %words_ref.1) | copy-start | bytes 6291460
  78.6 14.7 %collective-permute-start = (f16[2,512,256]{2,1,0:T(8,128)(2,1)S(1)}, f16[2,512,256]{2,1,0:T(8,128)(2,1)S(1)}, u32[]{:S(2)}, u32[]{:S(2)}) collective-permute-start(f16[2,512,256]{2,1,0:T(8,128)(2,1)S(1)} %convert_element_type.35), channel_id=1, source_target_pairs={{0,2},{1,3},{2,0},{3,1},{4,6},{5,7},{6,4},{7,5},{8,10},{9,11},{10,... | collective-permute-start | bytes 1572872 | tf_op jit(solution)/shard_map/ppermute | solution.py:218
  94.7 17.3 %all-to-all-start.5 = ((f16[64,4,512]{2,1,0:T(4,128)(2,1)}), f16[64,4,512]{2,1,0:T(4,128)(2,1)S(1)}, u32[]{:S(2)}, u32[]{:S(2)}) async-start(f16[64,4,512]{2,1,0:T(4,128)(2,1)} %convert_element_type.39), calls=%async_computation.5 | async-start | bytes 524288 | tf_op jit(solution)/shard_map/all_to_all | solution.py:182
  100.5 1.6 %collective-permute-start.1 = (f16[512,256]{1,0:T(8,128)(2,1)S(1)}, f16[512,256]{1,0:T(8,128)(2,1)S(1)}, u32[]{:S(2)}, u32[]{:S(2)}) collective-permute-start(f16[512,256]{1,0:T(8,128)(2,1)S(1)} %fusion), channel_id=1, source_target_pairs={{0,1},{1,0},{2,3},{3,2},{4,5},{5,4},{6,7},{7,6},{8,9},{9,8},{10,11... | collective-permute-start | bytes 786440 | tf_op jit(solution)/shard_map/ppermute | solution.py:223

commit v5 on v4

--- a/solution.py
+++ b/solution.py
@@ -159,7 +159,7 @@
                     at : at + WORDS, lane * 128 : (lane + 1) * 128
                 ]
     for lane in range(width // 128):
-        out_ref[:, lane * 128 : (lane + 1) * 128] = row_ref[lane] * scale
+        out_ref[:, lane * 128 : (lane + 1) * 128] = row_ref[lane, :quarter, :] * scale
 
     @pl.when(owned)
     def _():
@@ -226,7 +226,7 @@
         functools.partial(finish_kernel, 0.5 * rows ** (-0.5)),
         shape(quarter, width),
         [SCALARS, VECTORS, VECTORS, VECTORS],
-        [pltpu.VMEM((width // 128, quarter, 128), jnp.float32)],
+        [pltpu.VMEM((width // 128, quarter + PLANES, 128), jnp.float32)],
     )(owners, keep, far, back)
 
 

time: 114 us -> 114 us (level)
  no operation moved by 1% of the time
where the time goes in v5:
time: 114 us
  blocking collectives  79.4 us (70%)
  waiting for transfers between devices  11.4 us (10%)
  Pallas kernels  10.5 us (9%)
  starting transfers between devices  8.64 us (8%)
  local copies, waits for them, and re-layouts  1.89 us (2%)
  other arithmetic  1.61 us (1%)
    all_to_all x5, blocking collectives, swap(): return lax.all_to_all(value, 'blk', 0, 0, axis_index_groups=line)  79.4 us
    all_to_all x1, waiting for transfers between devices, swap(): return lax.all_to_all(value, 'blk', 0, 0, axis_index_groups=line)  9.92 us
    pallas_call x1, Pallas kernels, body(): local_call(products_kernel, (shape(2, quarter, width), shape(2, quarter,...  7.54 us
    all_to_all x1, starting transfers between devices, swap(): return lax.all_to_all(value, 'blk', 0, 0, axis_index_groups=line)  5.54 us
    ppermute x1, starting transfers between devices, body(): lax.ppermute(send.astype(jnp.float16), 'grp', [(g, g ^ 2) for g in range(...  3.01 us
  transfers between devices with their start and end apart: 3, of which 2 were waited for; matrix products, arithmetic and copies ran while one was open for 0% of the time, Pallas kernels for 0%

profile of v5, /device:TPU:32, one launch (start us, length us, event | category | flops | bytes accessed | tf_op | source)
XLA Modules:
  0.0 113.6 jit_solution(11822840429646336967)
XLA Ops:
  0.0 0.0 copy-start
  0.0 1.2 %copy-done = bf16[2048,256]{1,0:T(8,128)(2,1)S(1)} copy-done((bf16[2048,256]{1,0:T(8,128)(2,1)S(1)}, bf16[2048,256]{1,0:T(8,128)(2,1)}, u32[]{:S(2)}) %copy-start) | copy-done | bytes 1048600
  1.2 0.0 copy-start.2
  1.2 0.7 copy-done.2
  1.9 0.1 shard_map.37
  2.0 25.6 %all_to_all.30.got_ref = bf16[64,16,128]{2,1,0:T(8,128)(2,1)S(1)} all-to-all(bf16[64,16,128]{2,1,0:T(8,128)(2,1)S(1)} %get-tuple-element.17), channel_id=1, replica_groups=mesh['blk'=64,'grp'=4] {'blk'}, dimensions={0} | all-to-all | bytes 524288 | tf_op jit(solution)/shard_map/all_to_all | solution.py:182
  27.6 0.0 copy-start.1
  27.6 0.0 copy-start.3
  27.6 0.6 shard_map.38
  28.1 11.2 %all_to_all.31.came_ref = bf16[8,4,16,128]{3,2,1,0:T(8,128)(2,1)S(1)} all-to-all(bf16[8,4,16,128]{3,2,1,0:T(8,128)(2,1)S(1)} %shard_map.38), channel_id=1, replica_groups={{0,16,32,48,64,80,96,112},{4,20,36,52,68,84,100,116},{8,24,40,56,72,88,..., dimensions={0} | all-to-all | bytes 262144 | tf_op jit(solution)/shard_map/all_to_all | solution.py:182
  39.4 0.1 shard_map.39
  39.5 16.0 %all_to_all.32.pieces_ref = bf16[8,8,4,16,128]{4,3,2,1,0:T(8,128)(2,1)S(1)} all-to-all(bf16[8,8,4,16,128]{4,3,2,1,0:T(8,128)(2,1)S(1)} %shard_map.39), channel_id=1, replica_groups={{0,4,8,12,128,132,136,140},{16,20,24,28,144,148,152,156},{32,36,40,44,1..., dimensions={0} | all-to-all | bytes 2097152 | tf_op jit(solution)/shard_map/all_to_all | solution.py:182
  55.5 0.0 copy-done.1
  55.5 0.0 copy-done.3
  55.5 7.5 %shard_map.40 = (f32[2,512,256]{2,1,0:T(8,128)S(1)}, f32[2,512,256]{2,1,0:T(8,128)S(1)}, f32[256,2048]{1,0:T(8,128)S(1)}) custom-call(bf16[2048,256]{1,0:T(8,128)(2,1)S(1)} %copy-done.1, bf16[8,8,4,16,128]{4,3,2,1,0:T(8,128)(2,1)S(1)} %all_to_all.32.pieces_ref, s32[4,256,512]{2,1,0:T(8,128)S(1)} %copy-done.3), custom_call_target="tpu_custom_call" | custom-call | flops 6442450944 | bytes 9437184 | tf_op jit(solution)/shard_map/pallas_call | solution.py:201
  63.0 0.1 convert_element_type.31
  63.2 15.1 %all_to_all.33 = f16[8,32,2048]{2,1,0:T(8,128)(2,1)S(1)} all-to-all(f16[8,32,2048]{2,1,0:T(8,128)(2,1)S(1)} %bitcast.3), channel_id=1, replica_groups={{0,4,8,12,128,132,136,140},{16,20,24,28,144,148,152,156},{32,36,40,44,1..., dimensions={0} | all-to-all | bytes 2097152 | tf_op jit(solution)/shard_map/all_to_all | solution.py:182
  78.3 0.2 convert_element_type.32.came_ref
  78.5 0.1 convert_element_type.35
  78.6 3.0 %collective-permute-start = (f16[2,512,256]{2,1,0:T(8,128)(2,1)S(1)}, f16[2,512,256]{2,1,0:T(8,128)(2,1)S(1)}, u32[]{:S(2)}, u32[]{:S(2)}) collective-permute-start(f16[2,512,256]{2,1,0:T(8,128)(2,1)S(1)} %convert_element_type.35), channel_id=1, source_target_pairs={{0,2},{1,3},{2,0},{3,1},{4,6},{5,7},{6,4},{7,5},{8,10},{9,11},{10,... | collective-permute-start | bytes 1572872 | tf_op jit(solution)/shard_map/ppermute | solution.py:218
  81.6 0.1 shard_map.41
  81.8 11.5 %all_to_all.34 = f16[8,4,2048]{2,1,0:T(4,128)(2,1)S(1)} all-to-all(f16[8,4,2048]{2,1,0:T(4,128)(2,1)S(1)} %convert_element_type.33), channel_id=1, replica_groups={{0,16,32,48,64,80,96,112},{4,20,36,52,68,84,100,116},{8,24,40,56,72,88,..., dimensions={0} | all-to-all | bytes 262144 | tf_op jit(solution)/shard_map/all_to_all | solution.py:182
  93.3 0.0 collective-permute-done
  93.3 0.6 shard_map.42
  93.9 0.8 convert_element_type.39
  94.7 5.5 %all-to-all-start.5 = ((f16[64,4,512]{2,1,0:T(4,128)(2,1)}), f16[64,4,512]{2,1,0:T(4,128)(2,1)S(1)}, u32[]{:S(2)}, u32[]{:S(2)}) async-start(f16[64,4,512]{2,1,0:T(4,128)(2,1)} %convert_element_type.39), calls=%async_computation.5 | async-start | bytes 524288 | tf_op jit(solution)/shard_map/all_to_all | solution.py:182
  100.2 0.2 convert_add_fusion.keep_ref
  100.5 0.1 collective-permute-start.1
  100.6 1.5 %collective-permute-done.1 = f16[512,256]{1,0:T(8,128)(2,1)S(1)} collective-permute-done((f16[512,256]{1,0:T(8,128)(2,1)S(1)}, f16[512,256]{1,0:T(8,128)(2,1)S(1)}, u32[]{:S(2)}, u32[]{:S(2)}) %collective-permute-start.1) | collective-permute-done | bytes 262176 | tf_op jit(solution)/shard_map/ppermute | solution.py:223
  102.1 9.9 %all-to-all-done.5 = f16[64,4,512]{2,1,0:T(4,128)(2,1)S(1)} async-done(((f16[64,4,512]{2,1,0:T(4,128)(2,1)}), f16[64,4,512]{2,1,0:T(4,128)(2,1)S(1)}, u32[]{:S(2)}, u32[]{:S(2)}) %all-to-all-start.5) | async-done | bytes 262176 | tf_op jit(solution)/shard_map/all_to_all | solution.py:182
  112.0 0.1 convert_element_type.40.back_ref
  112.1 1.5 %shard_map.43 = f32[512,256]{1,0:T(8,128)} custom-call(s32[64]{0:T(128)S(1)} %get-tuple-element.16.owners_ref, f32[2,512,256]{2,1,0:T(8,128)S(1)} %convert_add_fusion.keep_ref, f32[512,256]{1,0:T(8,128)S(1)} %convert_element_type.38.came_ref, f32[64,4,512]{2,1,0:T(4,128)S(1)} %convert_element_type.40.back_ref), custom_call_target="tpu_custom_call" | custom-call | tf_op jit(solution)/shard_map/pallas_call | solution.py:225
  (4 shorter events, 0.2 us)
Async XLA Ops:
  0.0 1.2 %copy-start = (bf16[2048,256]{1,0:T(8,128)(2,1)S(1)}, bf16[2048,256]{1,0:T(8,128)(2,1)}, u32[]{:S(2)}) copy-start(bf16[2048,256]{1,0:T(8,128)(2,1)} %emb_ref.3) | copy-start | bytes 3145732
  1.2 0.7 copy-start.2
  27.6 27.9 %copy-start.1 = (bf16[2048,256]{1,0:T(8,128)(2,1)S(1)}, bf16[2048,256]{1,0:T(8,128)(2,1)}, u32[]{:S(2)}) copy-start(bf16[2048,256]{1,0:T(8,128)(2,1)} %emb_ref.3) | copy-start | bytes 3145732
  27.6 27.9 %copy-start.3 = (s32[4,256,512]{2,1,0:T(8,128)S(1)}, s32[4,256,512]{2,1,0:T(8,128)}, u32[]{:S(2)}) copy-start(s32[4,256,512]{2,1,0:T(8,128)} %words_ref.1) | copy-start | bytes 6291460
  78.6 14.7 %collective-permute-start = (f16[2,512,256]{2,1,0:T(8,128)(2,1)S(1)}, f16[2,512,256]{2,1,0:T(8,128)(2,1)S(1)}, u32[]{:S(2)}, u32[]{:S(2)}) collective-permute-start(f16[2,512,256]{2,1,0:T(8,128)(2,1)S(1)} %convert_element_type.35), channel_id=1, source_target_pairs={{0,2},{1,3},{2,0},{3,1},{4,6},{5,7},{6,4},{7,5},{8,10},{9,11},{10,... | collective-permute-start | bytes 1572872 | tf_op jit(solution)/shard_map/ppermute | solution.py:218
  94.7 17.3 %all-to-all-start.5 = ((f16[64,4,512]{2,1,0:T(4,128)(2,1)}), f16[64,4,512]{2,1,0:T(4,128)(2,1)S(1)}, u32[]{:S(2)}, u32[]{:S(2)}) async-start(f16[64,4,512]{2,1,0:T(4,128)(2,1)} %convert_element_type.39), calls=%async_computation.5 | async-start | bytes 524288 | tf_op jit(solution)/shard_map/all_to_all | solution.py:182
  100.5 1.6 %collective-permute-start.1 = (f16[512,256]{1,0:T(8,128)(2,1)S(1)}, f16[512,256]{1,0:T(8,128)(2,1)S(1)}, u32[]{:S(2)}, u32[]{:S(2)}) collective-permute-start(f16[512,256]{1,0:T(8,128)(2,1)S(1)} %fusion), channel_id=1, source_target_pairs={{0,1},{1,0},{2,3},{3,2},{4,5},{5,4},{6,7},{7,6},{8,9},{9,8},{10,11... | collective-permute-start | bytes 786440 | tf_op jit(solution)/shard_map/ppermute | solution.py:223

commit v6 on v5

--- a/solution.py
+++ b/solution.py
@@ -144,13 +144,9 @@
         out_ref[owners_ref[s]] = total[:, s * quarter : (s + 1) * quarter] * 0.125
 
 
-def finish_kernel(scale, owners_ref, keep_ref, came_ref, back_ref, out_ref, row_ref):
-    mine = lax.axis_index("blk")
-    owned = jnp.bool_(False)
-    for s in range(SECTIONS):
-        owned = owned | (owners_ref[s] == mine)
+def rows_kernel(scale, keep_ref, came_ref, out_ref, row_ref):
     quarter, width = out_ref.shape
-    row = keep_ref[0] + came_ref[...].astype(jnp.float32)
+    row = keep_ref[0] + came_ref[...]
     for tile in range(quarter // TILE):
         for plane in range(PLANES):
             at = tile * TILE + plane * WORDS
@@ -161,9 +157,21 @@
     for lane in range(width // 128):
         out_ref[:, lane * 128 : (lane + 1) * 128] = row_ref[lane, :quarter, :] * scale
 
+
+def finish_kernel(scale, owners_ref, rows_ref, back_ref, out_ref):
+    mine = lax.axis_index("blk")
+    owned = jnp.bool_(False)
+    for s in range(SECTIONS):
+        owned = owned | (owners_ref[s] == mine)
+    quarter, width = out_ref.shape
+
     @pl.when(owned)
     def _():
-        out_ref[...] += back_ref[...].reshape(width, quarter).T * (8.0 * scale)
+        out_ref[...] = rows_ref[...] + back_ref[...].reshape(width, quarter).T * (8.0 * scale)
+
+    @pl.when(jnp.logical_not(owned))
+    def _():
+        out_ref[...] = rows_ref[...]
 
 
 def body(embedding, adjacency, owners):
@@ -222,12 +230,16 @@
     col = local_call(to_owner_kernel, shape(blocks, width // blocks, quarter), [SCALARS, VECTORS])(owners, col)
     far = lax.ppermute(keep[1].astype(jnp.float16), "grp", [(g, g ^ 1) for g in range(groups)]).astype(jnp.float32)
     back = swap(col.astype(jnp.float16)).astype(jnp.float32)
-    return local_call(
-        functools.partial(finish_kernel, 0.5 * rows ** (-0.5)),
+    scale = 0.5 * rows ** (-0.5)
+    row = local_call(
+        functools.partial(rows_kernel, scale),
         shape(quarter, width),
-        [SCALARS, VECTORS, VECTORS, VECTORS],
+        [VECTORS] * 2,
         [pltpu.VMEM((width // 128, quarter + PLANES, 128), jnp.float32)],
-    )(owners, keep, far, back)
+    )(keep, far)
+    return local_call(functools.partial(finish_kernel, scale), shape(quarter, width), [SCALARS, VECTORS, VECTORS])(
+        owners, row, back
+    )
 
 
 def solution(mesh):

time: 114 us -> 114 us (level)
  no operation moved by 1% of the time
where the time goes in v6:
time: 114 us
  blocking collectives  79.4 us (70%)
  waiting for transfers between devices  11.3 us (10%)
  Pallas kernels  10.7 us (9%)
  starting transfers between devices  8.64 us (8%)
  local copies, waits for them, and re-layouts  1.89 us (2%)
  other arithmetic  1.61 us (1%)
    all_to_all x5, blocking collectives, swap(): return lax.all_to_all(value, 'blk', 0, 0, axis_index_groups=line)  79.4 us
    all_to_all x1, waiting for transfers between devices, swap(): return lax.all_to_all(value, 'blk', 0, 0, axis_index_groups=line)  9.74 us
    pallas_call x1, Pallas kernels, body(): local_call(products_kernel, (shape(2, quarter, width), shape(2, quarter,...  7.54 us
    all_to_all x1, starting transfers between devices, swap(): return lax.all_to_all(value, 'blk', 0, 0, axis_index_groups=line)  5.54 us
    ppermute x1, starting transfers between devices, body(): lax.ppermute(send.astype(jnp.float16), 'grp', [(g, g ^ 2) for g in range(...  3.01 us
  transfers between devices with their start and end apart: 3, of which 2 were waited for; matrix products, arithmetic and copies ran while one was open for 0% of the time, Pallas kernels for 0%

profile of v6, /device:TPU:32, one launch (start us, length us, event | category | flops | bytes accessed | tf_op | source)
XLA Modules:
  0.0 113.7 jit_solution(15194420234221032208)
XLA Ops:
  0.0 0.0 copy-start
  0.0 1.2 %copy-done = bf16[2048,256]{1,0:T(8,128)(2,1)S(1)} copy-done((bf16[2048,256]{1,0:T(8,128)(2,1)S(1)}, bf16[2048,256]{1,0:T(8,128)(2,1)}, u32[]{:S(2)}) %copy-start) | copy-done | bytes 1048600
  1.2 0.0 copy-start.2
  1.2 0.7 copy-done.2
  1.9 0.1 shard_map.37
  2.0 25.6 %all_to_all.30.got_ref = bf16[64,16,128]{2,1,0:T(8,128)(2,1)S(1)} all-to-all(bf16[64,16,128]{2,1,0:T(8,128)(2,1)S(1)} %get-tuple-element.17), channel_id=1, replica_groups=mesh['blk'=64,'grp'=4] {'blk'}, dimensions={0} | all-to-all | bytes 524288 | tf_op jit(solution)/shard_map/all_to_all | solution.py:190
  27.6 0.0 copy-start.1
  27.6 0.0 copy-start.3
  27.6 0.6 shard_map.38
  28.1 11.2 %all_to_all.31.came_ref = bf16[8,4,16,128]{3,2,1,0:T(8,128)(2,1)S(1)} all-to-all(bf16[8,4,16,128]{3,2,1,0:T(8,128)(2,1)S(1)} %shard_map.38), channel_id=1, replica_groups={{0,16,32,48,64,80,96,112},{4,20,36,52,68,84,100,116},{8,24,40,56,72,88,..., dimensions={0} | all-to-all | bytes 262144 | tf_op jit(solution)/shard_map/all_to_all | solution.py:190
  39.4 0.1 shard_map.39
  39.5 16.0 %all_to_all.32.pieces_ref = bf16[8,8,4,16,128]{4,3,2,1,0:T(8,128)(2,1)S(1)} all-to-all(bf16[8,8,4,16,128]{4,3,2,1,0:T(8,128)(2,1)S(1)} %shard_map.39), channel_id=1, replica_groups={{0,4,8,12,128,132,136,140},{16,20,24,28,144,148,152,156},{32,36,40,44,1..., dimensions={0} | all-to-all | bytes 2097152 | tf_op jit(solution)/shard_map/all_to_all | solution.py:190
  55.5 0.0 copy-done.1
  55.5 0.0 copy-done.3
  55.5 7.5 %shard_map.40 = (f32[2,512,256]{2,1,0:T(8,128)S(1)}, f32[2,512,256]{2,1,0:T(8,128)S(1)}, f32[256,2048]{1,0:T(8,128)S(1)}) custom-call(bf16[2048,256]{1,0:T(8,128)(2,1)S(1)} %copy-done.1, bf16[8,8,4,16,128]{4,3,2,1,0:T(8,128)(2,1)S(1)} %all_to_all.32.pieces_ref, s32[4,256,512]{2,1,0:T(8,128)S(1)} %copy-done.3), custom_call_target="tpu_custom_call" | custom-call | flops 6442450944 | bytes 9437184 | tf_op jit(solution)/shard_map/pallas_call | solution.py:209
  63.0 0.1 convert_element_type.31
  63.2 15.1 %all_to_all.33 = f16[8,32,2048]{2,1,0:T(8,128)(2,1)S(1)} all-to-all(f16[8,32,2048]{2,1,0:T(8,128)(2,1)S(1)} %bitcast.3), channel_id=1, replica_groups={{0,4,8,12,128,132,136,140},{16,20,24,28,144,148,152,156},{32,36,40,44,1..., dimensions={0} | all-to-all | bytes 2097152 | tf_op jit(solution)/shard_map/all_to_all | solution.py:190
  78.3 0.2 convert_element_type.32.came_ref
  78.5 0.1 convert_element_type.35
  78.6 3.0 %collective-permute-start = (f16[2,512,256]{2,1,0:T(8,128)(2,1)S(1)}, f16[2,512,256]{2,1,0:T(8,128)(2,1)S(1)}, u32[]{:S(2)}, u32[]{:S(2)}) collective-permute-start(f16[2,512,256]{2,1,0:T(8,128)(2,1)S(1)} %convert_element_type.35), channel_id=1, source_target_pairs={{0,2},{1,3},{2,0},{3,1},{4,6},{5,7},{6,4},{7,5},{8,10},{9,11},{10,... | collective-permute-start | bytes 1572872 | tf_op jit(solution)/shard_map/ppermute | solution.py:226
  81.6 0.1 shard_map.41
  81.8 11.5 %all_to_all.34 = f16[8,4,2048]{2,1,0:T(4,128)(2,1)S(1)} all-to-all(f16[8,4,2048]{2,1,0:T(4,128)(2,1)S(1)} %convert_element_type.33), channel_id=1, replica_groups={{0,16,32,48,64,80,96,112},{4,20,36,52,68,84,100,116},{8,24,40,56,72,88,..., dimensions={0} | all-to-all | bytes 262144 | tf_op jit(solution)/shard_map/all_to_all | solution.py:190
  93.3 0.0 collective-permute-done
  93.3 0.6 shard_map.43
  93.9 0.8 convert_element_type.39
  94.7 5.5 %all-to-all-start.5 = ((f16[64,4,512]{2,1,0:T(4,128)(2,1)}), f16[64,4,512]{2,1,0:T(4,128)(2,1)S(1)}, u32[]{:S(2)}, u32[]{:S(2)}) async-start(f16[64,4,512]{2,1,0:T(4,128)(2,1)} %convert_element_type.39), calls=%async_computation.5 | async-start | bytes 524288 | tf_op jit(solution)/shard_map/all_to_all | solution.py:190
  100.2 0.2 convert_add_fusion.keep_ref
  100.5 0.1 collective-permute-start.1
  100.6 1.5 %collective-permute-done.1 = f16[512,256]{1,0:T(8,128)(2,1)S(1)} collective-permute-done((f16[512,256]{1,0:T(8,128)(2,1)S(1)}, f16[512,256]{1,0:T(8,128)(2,1)S(1)}, u32[]{:S(2)}, u32[]{:S(2)}) %collective-permute-start.1) | collective-permute-done | bytes 262176 | tf_op jit(solution)/shard_map/ppermute | solution.py:231
  102.1 0.2 shard_map.42.rows_ref
  102.3 9.7 %all-to-all-done.5 = f16[64,4,512]{2,1,0:T(4,128)(2,1)S(1)} async-done(((f16[64,4,512]{2,1,0:T(4,128)(2,1)}), f16[64,4,512]{2,1,0:T(4,128)(2,1)S(1)}, u32[]{:S(2)}, u32[]{:S(2)}) %all-to-all-start.5) | async-done | bytes 262176 | tf_op jit(solution)/shard_map/all_to_all | solution.py:190
  112.0 0.1 convert_element_type.40.back_ref
  112.1 1.6 %shard_map.44 = f32[512,256]{1,0:T(8,128)} custom-call(s32[64]{0:T(128)S(1)} %get-tuple-element.16.owners_ref, f32[512,256]{1,0:T(8,128)S(1)} %shard_map.42.rows_ref, f32[64,4,512]{2,1,0:T(4,128)S(1)} %convert_element_type.40.back_ref), custom_call_target="tpu_custom_call" | custom-call | tf_op jit(solution)/shard_map/pallas_call | solution.py:240
  (4 shorter events, 0.2 us)
Async XLA Ops:
  0.0 1.2 %copy-start = (bf16[2048,256]{1,0:T(8,128)(2,1)S(1)}, bf16[2048,256]{1,0:T(8,128)(2,1)}, u32[]{:S(2)}) copy-start(bf16[2048,256]{1,0:T(8,128)(2,1)} %emb_ref.3) | copy-start | bytes 3145732
  1.2 0.7 copy-start.2
  27.6 27.9 %copy-start.1 = (bf16[2048,256]{1,0:T(8,128)(2,1)S(1)}, bf16[2048,256]{1,0:T(8,128)(2,1)}, u32[]{:S(2)}) copy-start(bf16[2048,256]{1,0:T(8,128)(2,1)} %emb_ref.3) | copy-start | bytes 3145732
  27.6 27.9 %copy-start.3 = (s32[4,256,512]{2,1,0:T(8,128)S(1)}, s32[4,256,512]{2,1,0:T(8,128)}, u32[]{:S(2)}) copy-start(s32[4,256,512]{2,1,0:T(8,128)} %words_ref.1) | copy-start | bytes 6291460
  78.6 14.7 %collective-permute-start = (f16[2,512,256]{2,1,0:T(8,128)(2,1)S(1)}, f16[2,512,256]{2,1,0:T(8,128)(2,1)S(1)}, u32[]{:S(2)}, u32[]{:S(2)}) collective-permute-start(f16[2,512,256]{2,1,0:T(8,128)(2,1)S(1)} %convert_element_type.35), channel_id=1, source_target_pairs={{0,2},{1,3},{2,0},{3,1},{4,6},{5,7},{6,4},{7,5},{8,10},{9,11},{10,... | collective-permute-start | bytes 1572872 | tf_op jit(solution)/shard_map/ppermute | solution.py:226
  94.7 17.3 %all-to-all-start.5 = ((f16[64,4,512]{2,1,0:T(4,128)(2,1)}), f16[64,4,512]{2,1,0:T(4,128)(2,1)S(1)}, u32[]{:S(2)}, u32[]{:S(2)}) async-start(f16[64,4,512]{2,1,0:T(4,128)(2,1)} %convert_element_type.39), calls=%async_computation.5 | async-start | bytes 524288 | tf_op jit(solution)/shard_map/all_to_all | solution.py:190
  100.5 1.6 %collective-permute-start.1 = (f16[512,256]{1,0:T(8,128)(2,1)S(1)}, f16[512,256]{1,0:T(8,128)(2,1)S(1)}, u32[]{:S(2)}, u32[]{:S(2)}) collective-permute-start(f16[512,256]{1,0:T(8,128)(2,1)S(1)} %fusion), channel_id=1, source_target_pairs={{0,1},{1,0},{2,3},{3,2},{4,5},{5,4},{6,7},{7,6},{8,9},{9,8},{10,11... | collective-permute-start | bytes 786440 | tf_op jit(solution)/shard_map/ppermute | solution.py:231

commit v7 on v6

--- a/solution.py
+++ b/solution.py
@@ -99,24 +99,37 @@
         cols_ref[:, span] = lax.dot_general(
             spread, here, (((1,), (1,)), ((), ())), preferred_element_type=jnp.float32
         ).astype(jnp.bfloat16)
-    for pair in range(4):
+
+    def scores_of(pair, section):
+        return lax.dot_general(
+            rows_ref[pair * 2 * TILE : (pair + 1) * 2 * TILE, :],
+            block_ref[section * quarter : (section + 1) * quarter, :],
+            (((1,), (1,)), ((), ())),
+            preferred_element_type=jnp.float32,
+        )
+
+    def write_rows(pair):
         span = slice(pair * 2 * TILE, (pair + 1) * 2 * TILE)
-        for section in range(sections):
-            cut = slice(section * quarter, (section + 1) * quarter)
-            scores = lax.dot_general(
-                rows_ref[span, :], block_ref[cut, :], (((1,), (1,)), ((), ())), preferred_element_type=jnp.float32
-            )
-            for sub in range(2):
-                tile = tiles[pair * 2 + sub]
-                words = words_ref[section, pl.ds(pl.multiple_of(tile * WORDS, WORDS), WORDS), :]
-                for plane in range(PLANES):
-                    at = sub * TILE + plane * WORDS
-                    sign = jnp.where((words & (1 << plane)) == 0, 1.0, -1.0)
-                    error = jnp.tanh(scores[at : at + WORDS, :]) + sign
-                    error_ref[pair * 2 * TILE + at : pair * 2 * TILE + at + WORDS, cut] = error.astype(jnp.bfloat16)
-        row = jnp.dot(error_ref[span, :], block_ref[...], preferred_element_type=jnp.float32)
         store = keep_ref if pair // 2 else send_ref
-        store[pair % 2] = row
+        store[pair % 2] = jnp.dot(error_ref[span, :], block_ref[...], preferred_element_type=jnp.float32)
+
+    steps = [(pair, section) for pair in range(4) for section in range(sections)]
+    scores = scores_of(*steps[0])
+    for step, (pair, section) in enumerate(steps):
+        following = scores_of(*steps[step + 1]) if step + 1 < len(steps) else None
+        if pair > 0 and section == 0:
+            write_rows(pair - 1)
+        cut = slice(section * quarter, (section + 1) * quarter)
+        for sub in range(2):
+            tile = tiles[pair * 2 + sub]
+            words = words_ref[section, pl.ds(pl.multiple_of(tile * WORDS, WORDS), WORDS), :]
+            for plane in range(PLANES):
+                at = sub * TILE + plane * WORDS
+                sign = jnp.where((words & (1 << plane)) == 0, 1.0, -1.0)
+                error = jnp.tanh(scores[at : at + WORDS, :]) + sign
+                error_ref[pair * 2 * TILE + at : pair * 2 * TILE + at + WORDS, cut] = error.astype(jnp.bfloat16)
+        scores = following
+    write_rows(3)
     for section in range(sections):
         cut = slice(section * quarter, (section + 1) * quarter)
         col_ref[:, cut] = jnp.dot(cols_ref[...], error_ref[:, cut], preferred_element_type=jnp.float32)

time: 114 us -> 114 us (level)
  no operation moved by 1% of the time
where the time goes in v7:
time: 114 us
  blocking collectives  79.4 us (70%)
  waiting for transfers between devices  11.3 us (10%)
  Pallas kernels  10.6 us (9%)
  starting transfers between devices  8.64 us (8%)
  local copies, waits for them, and re-layouts  1.89 us (2%)
  other arithmetic  1.61 us (1%)
    all_to_all x5, blocking collectives, swap(): return lax.all_to_all(value, 'blk', 0, 0, axis_index_groups=line)  79.4 us
    all_to_all x1, waiting for transfers between devices, swap(): return lax.all_to_all(value, 'blk', 0, 0, axis_index_groups=line)  9.74 us
    pallas_call x1, Pallas kernels, body(): local_call(products_kernel, (shape(2, quarter, width), shape(2, quarter,...  7.55 us
    all_to_all x1, starting transfers between devices, swap(): return lax.all_to_all(value, 'blk', 0, 0, axis_index_groups=line)  5.54 us
    ppermute x1, starting transfers between devices, body(): lax.ppermute(send.astype(jnp.float16), 'grp', [(g, g ^ 2) for g in range(...  3.01 us
  transfers between devices with their start and end apart: 3, of which 2 were waited for; matrix products, arithmetic and copies ran while one was open for 0% of the time, Pallas kernels for 0%

profile of v7, /device:TPU:32, one launch (start us, length us, event | category | flops | bytes accessed | tf_op | source)
XLA Modules:
  0.0 113.5 jit_solution(4260742075184443076)
XLA Ops:
  0.0 0.0 copy-start
  0.0 1.2 %copy-done = bf16[2048,256]{1,0:T(8,128)(2,1)S(1)} copy-done((bf16[2048,256]{1,0:T(8,128)(2,1)S(1)}, bf16[2048,256]{1,0:T(8,128)(2,1)}, u32[]{:S(2)}) %copy-start) | copy-done | bytes 1048600
  1.2 0.0 copy-start.2
  1.2 0.7 copy-done.2
  1.9 0.1 shard_map.37
  2.0 25.6 %all_to_all.30.got_ref = bf16[64,16,128]{2,1,0:T(8,128)(2,1)S(1)} all-to-all(bf16[64,16,128]{2,1,0:T(8,128)(2,1)S(1)} %get-tuple-element.17), channel_id=1, replica_groups=mesh['blk'=64,'grp'=4] {'blk'}, dimensions={0} | all-to-all | bytes 524288 | tf_op jit(solution)/shard_map/all_to_all | solution.py:203
  27.6 0.0 copy-start.1
  27.6 0.0 copy-start.3
  27.6 0.6 shard_map.38
  28.1 11.2 %all_to_all.31.came_ref = bf16[8,4,16,128]{3,2,1,0:T(8,128)(2,1)S(1)} all-to-all(bf16[8,4,16,128]{3,2,1,0:T(8,128)(2,1)S(1)} %shard_map.38), channel_id=1, replica_groups={{0,16,32,48,64,80,96,112},{4,20,36,52,68,84,100,116},{8,24,40,56,72,88,..., dimensions={0} | all-to-all | bytes 262144 | tf_op jit(solution)/shard_map/all_to_all | solution.py:203
  39.4 0.1 shard_map.39
  39.5 16.0 %all_to_all.32.pieces_ref = bf16[8,8,4,16,128]{4,3,2,1,0:T(8,128)(2,1)S(1)} all-to-all(bf16[8,8,4,16,128]{4,3,2,1,0:T(8,128)(2,1)S(1)} %shard_map.39), channel_id=1, replica_groups={{0,4,8,12,128,132,136,140},{16,20,24,28,144,148,152,156},{32,36,40,44,1..., dimensions={0} | all-to-all | bytes 2097152 | tf_op jit(solution)/shard_map/all_to_all | solution.py:203
  55.5 0.0 copy-done.1
  55.5 0.0 copy-done.3
  55.5 7.5 %shard_map.40 = (f32[2,512,256]{2,1,0:T(8,128)S(1)}, f32[2,512,256]{2,1,0:T(8,128)S(1)}, f32[256,2048]{1,0:T(8,128)S(1)}) custom-call(bf16[2048,256]{1,0:T(8,128)(2,1)S(1)} %copy-done.1, bf16[8,8,4,16,128]{4,3,2,1,0:T(8,128)(2,1)S(1)} %all_to_all.32.pieces_ref, s32[4,256,512]{2,1,0:T(8,128)S(1)} %copy-done.3), custom_call_target="tpu_custom_call" | custom-call | flops 6442450944 | bytes 9437184 | tf_op jit(solution)/shard_map/pallas_call | solution.py:222
  63.1 0.1 convert_element_type.31
  63.2 15.1 %all_to_all.33 = f16[8,32,2048]{2,1,0:T(8,128)(2,1)S(1)} all-to-all(f16[8,32,2048]{2,1,0:T(8,128)(2,1)S(1)} %bitcast.3), channel_id=1, replica_groups={{0,4,8,12,128,132,136,140},{16,20,24,28,144,148,152,156},{32,36,40,44,1..., dimensions={0} | all-to-all | bytes 2097152 | tf_op jit(solution)/shard_map/all_to_all | solution.py:203
  78.4 0.2 convert_element_type.32.came_ref
  78.5 0.1 convert_element_type.35
  78.6 3.0 %collective-permute-start = (f16[2,512,256]{2,1,0:T(8,128)(2,1)S(1)}, f16[2,512,256]{2,1,0:T(8,128)(2,1)S(1)}, u32[]{:S(2)}, u32[]{:S(2)}) collective-permute-start(f16[2,512,256]{2,1,0:T(8,128)(2,1)S(1)} %convert_element_type.35), channel_id=1, source_target_pairs={{0,2},{1,3},{2,0},{3,1},{4,6},{5,7},{6,4},{7,5},{8,10},{9,11},{10,... | collective-permute-start | bytes 1572872 | tf_op jit(solution)/shard_map/ppermute | solution.py:239
  81.6 0.1 shard_map.41
  81.8 11.5 %all_to_all.34 = f16[8,4,2048]{2,1,0:T(4,128)(2,1)S(1)} all-to-all(f16[8,4,2048]{2,1,0:T(4,128)(2,1)S(1)} %convert_element_type.33), channel_id=1, replica_groups={{0,16,32,48,64,80,96,112},{4,20,36,52,68,84,100,116},{8,24,40,56,72,88,..., dimensions={0} | all-to-all | bytes 262144 | tf_op jit(solution)/shard_map/all_to_all | solution.py:203
  93.3 0.0 collective-permute-done
  93.3 0.6 shard_map.43
  93.9 0.8 convert_element_type.39
  94.7 5.5 %all-to-all-start.5 = ((f16[64,4,512]{2,1,0:T(4,128)(2,1)}), f16[64,4,512]{2,1,0:T(4,128)(2,1)S(1)}, u32[]{:S(2)}, u32[]{:S(2)}) async-start(f16[64,4,512]{2,1,0:T(4,128)(2,1)} %convert_element_type.39), calls=%async_computation.5 | async-start | bytes 524288 | tf_op jit(solution)/shard_map/all_to_all | solution.py:203
  100.3 0.2 convert_add_fusion.keep_ref
  100.5 0.1 collective-permute-start.1
  100.6 1.5 %collective-permute-done.1 = f16[512,256]{1,0:T(8,128)(2,1)S(1)} collective-permute-done((f16[512,256]{1,0:T(8,128)(2,1)S(1)}, f16[512,256]{1,0:T(8,128)(2,1)S(1)}, u32[]{:S(2)}, u32[]{:S(2)}) %collective-permute-start.1) | collective-permute-done | bytes 262176 | tf_op jit(solution)/shard_map/ppermute | solution.py:244
  102.1 0.2 shard_map.42.rows_ref
  102.3 9.7 %all-to-all-done.5 = f16[64,4,512]{2,1,0:T(4,128)(2,1)S(1)} async-done(((f16[64,4,512]{2,1,0:T(4,128)(2,1)}), f16[64,4,512]{2,1,0:T(4,128)(2,1)S(1)}, u32[]{:S(2)}, u32[]{:S(2)}) %all-to-all-start.5) | async-done | bytes 262176 | tf_op jit(solution)/shard_map/all_to_all | solution.py:203
  112.0 0.1 convert_element_type.40.back_ref
  112.1 1.4 %shard_map.44 = f32[512,256]{1,0:T(8,128)} custom-call(s32[64]{0:T(128)S(1)} %get-tuple-element.16.owners_ref, f32[512,256]{1,0:T(8,128)S(1)} %shard_map.42.rows_ref, f32[64,4,512]{2,1,0:T(4,128)S(1)} %convert_element_type.40.back_ref), custom_call_target="tpu_custom_call" | custom-call | tf_op jit(solution)/shard_map/pallas_call | solution.py:253
  (4 shorter events, 0.2 us)
Async XLA Ops:
  0.0 1.2 %copy-start = (bf16[2048,256]{1,0:T(8,128)(2,1)S(1)}, bf16[2048,256]{1,0:T(8,128)(2,1)}, u32[]{:S(2)}) copy-start(bf16[2048,256]{1,0:T(8,128)(2,1)} %emb_ref.3) | copy-start | bytes 3145732
  1.2 0.7 copy-start.2
  27.6 27.9 %copy-start.1 = (bf16[2048,256]{1,0:T(8,128)(2,1)S(1)}, bf16[2048,256]{1,0:T(8,128)(2,1)}, u32[]{:S(2)}) copy-start(bf16[2048,256]{1,0:T(8,128)(2,1)} %emb_ref.3) | copy-start | bytes 3145732
  27.6 27.9 %copy-start.3 = (s32[4,256,512]{2,1,0:T(8,128)S(1)}, s32[4,256,512]{2,1,0:T(8,128)}, u32[]{:S(2)}) copy-start(s32[4,256,512]{2,1,0:T(8,128)} %words_ref.1) | copy-start | bytes 6291460
  78.6 14.7 %collective-permute-start = (f16[2,512,256]{2,1,0:T(8,128)(2,1)S(1)}, f16[2,512,256]{2,1,0:T(8,128)(2,1)S(1)}, u32[]{:S(2)}, u32[]{:S(2)}) collective-permute-start(f16[2,512,256]{2,1,0:T(8,128)(2,1)S(1)} %convert_element_type.35), channel_id=1, source_target_pairs={{0,2},{1,3},{2,0},{3,1},{4,6},{5,7},{6,4},{7,5},{8,10},{9,11},{10,... | collective-permute-start | bytes 1572872 | tf_op jit(solution)/shard_map/ppermute | solution.py:239
  94.7 17.3 %all-to-all-start.5 = ((f16[64,4,512]{2,1,0:T(4,128)(2,1)}), f16[64,4,512]{2,1,0:T(4,128)(2,1)S(1)}, u32[]{:S(2)}, u32[]{:S(2)}) async-start(f16[64,4,512]{2,1,0:T(4,128)(2,1)} %convert_element_type.39), calls=%async_computation.5 | async-start | bytes 524288 | tf_op jit(solution)/shard_map/all_to_all | solution.py:203
  100.5 1.6 %collective-permute-start.1 = (f16[512,256]{1,0:T(8,128)(2,1)S(1)}, f16[512,256]{1,0:T(8,128)(2,1)S(1)}, u32[]{:S(2)}, u32[]{:S(2)}) collective-permute-start(f16[512,256]{1,0:T(8,128)(2,1)S(1)} %fusion), channel_id=1, source_target_pairs={{0,1},{1,0},{2,3},{3,2},{4,5},{5,4},{6,7},{7,6},{8,9},{9,8},{10,11... | collective-permute-start | bytes 786440 | tf_op jit(solution)/shard_map/ppermute | solution.py:244
